TPU v7x, 32 devices: a whole 2x2x4 slice. The times are simulated.
32 devices in a mesh: grp: 4 (over x, core), dev: 8 (over z, y).
Axes of the slice: x: 2, y: 2, z: 4, core: 2. Of those that a mesh axis runs over, the one named last changes fastest.
Arguments:
- amplitudes: float32 [2, 2048, 128], P(None, ('grp', 'dev')), may hold values from -6 to 6
- couplings: float32 [2, 12, 128, 128], replicated, may hold values from -1 to 1, as said below
- block_index: int32 [128], P(('grp', 'dev')), may hold values from 0 to 11
- bond_map: int32 [5], replicated, may hold values from 0 to 6
- bond_strength: float32 [5], replicated, may hold values from 0.05 to 0.5
- drive_amplitude: float32 [4, 5], replicated, may hold values from 0.05 to 0.5
Outputs:
- new_amplitudes: float32 [2, 2048, 128], P(None, ('grp', 'dev'))
Inputs may be any that keep to these rules, and one draw needn't show every extreme that they name: couplings[0][k] is symmetric and couplings[1][k] antisymmetric, so each listed coupling is Hermitian.
All inputs are finite; a program needn't handle non-finite values.
Results may differ from a plain program's by a relative error of at most 0.00007.
Values sent between devices are 32-bit elements; how exact they have to be, the bound alone decides.
A program may use at most 64 MiB of HBM per device.

v0:
```python
import jax
import jax.numpy as jnp
from jax import lax
from jax.sharding import PartitionSpec as P

BROWS = 16


STEP_SIZE = 0.5
HIGHEST = lax.Precision.HIGHEST


def swapped(shard, axis, distance):
    return lax.ppermute(shard, axis, [(i, i ^ 1 << distance) for i in range(lax.axis_size(axis))])


def spin_count(number):
    return number.bit_length() - 1


def flip_group(real_part, imag_part, bit_now):
    return swapped((real_part, imag_part), "grp", bit_now)


def coupled(real_part, imag_part, table, row_kind, kinds):
    row_count, col_count = real_part.shape
    product = jnp.dot(
        jnp.concatenate([real_part, imag_part], 0),
        table,
        precision=HIGHEST,
        preferred_element_type=jnp.float32,
    )
    extent = kinds * col_count
    left_part = product[:, :extent]
    right_part = product[:, extent:]
    all_real = left_part[:row_count] - right_part[row_count:]
    all_imag = left_part[row_count:] + right_part[:row_count]
    select = (row_kind[:, None] == jnp.arange(kinds, dtype=jnp.int32)[None, :]).astype(jnp.float32)[
        :, :, None
    ]
    out_real = jnp.sum(all_real.reshape(row_count, kinds, col_count) * select, axis=1)
    out_imag = jnp.sum(all_imag.reshape(row_count, kinds, col_count) * select, axis=1)
    return (out_real, out_imag)


def evaluate_field(
    real_part, imag_part, table, row_kind, kinds, bond_map, bond_strength, drive_row
):
    out_real, out_imag = coupled(real_part, imag_part, table, row_kind, kinds)
    row_count, col_count = real_part.shape
    dev_bits = spin_count(lax.axis_size("dev"))
    grp_bits = spin_count(lax.axis_size("grp"))
    columns = jnp.arange(col_count, dtype=jnp.int32)
    for lead_spin in range(dev_bits + grp_bits):
        target = bond_map[lead_spin]
        shuffle = jnp.bitwise_xor(columns, jnp.left_shift(jnp.int32(1), target))
        sign_col = (1 - 2 * jnp.bitwise_and(jnp.right_shift(columns, target), 1)).astype(
            jnp.float32
        )[None, :]
        if lead_spin < dev_bits:
            part_real, part_imag = swapped((real_part, imag_part), "dev", lead_spin)
            sign_lead = (
                1 - 2 * jnp.bitwise_and(jnp.right_shift(lax.axis_index("dev"), lead_spin), 1)
            ).astype(jnp.float32)
        else:
            part_real, part_imag = flip_group(real_part, imag_part, lead_spin - dev_bits)
            sign_lead = (
                1
                - 2
                * jnp.bitwise_and(jnp.right_shift(lax.axis_index("grp"), lead_spin - dev_bits), 1)
            ).astype(jnp.float32)
        strength = bond_strength[lead_spin]
        drive_now = drive_row[lead_spin]
        out_real = (
            out_real
            + strength * (sign_lead * sign_col * real_part + jnp.take(part_real, shuffle, axis=1))
            + drive_now * part_real
        )
        out_imag = (
            out_imag
            + strength * (sign_lead * sign_col * imag_part + jnp.take(part_imag, shuffle, axis=1))
            + drive_now * part_imag
        )
    return (out_imag, -out_real)


def runge_kutta(real_part, imag_part, evaluate):
    half_step = 0.5 * STEP_SIZE
    slope_one = evaluate(0, real_part, imag_part)
    slope_two = evaluate(
        1, real_part + half_step * slope_one[0], imag_part + half_step * slope_one[1]
    )
    slope_three = evaluate(
        2, real_part + half_step * slope_two[0], imag_part + half_step * slope_two[1]
    )
    slope_four = evaluate(
        3, real_part + STEP_SIZE * slope_three[0], imag_part + STEP_SIZE * slope_three[1]
    )
    factor = STEP_SIZE / 6.0
    new_real = real_part + factor * (
        slope_one[0] + 2.0 * slope_two[0] + 2.0 * slope_three[0] + slope_four[0]
    )
    new_imag = imag_part + factor * (
        slope_one[1] + 2.0 * slope_two[1] + 2.0 * slope_three[1] + slope_four[1]
    )
    return (new_real, new_imag)


def body(amplitudes, couplings, block_index, bond_map, bond_strength, drive_amplitude):
    kinds = couplings.shape[1]
    col_count = couplings.shape[2]
    table_real = jnp.transpose(couplings[0], (2, 0, 1)).reshape(col_count, kinds * col_count)
    table_imag = jnp.transpose(couplings[1], (2, 0, 1)).reshape(col_count, kinds * col_count)
    table = jnp.concatenate([table_real, table_imag], 1)
    real_part = amplitudes[0]
    imag_part = amplitudes[1]
    row_count = real_part.shape[0]
    row_kind = jnp.repeat(block_index, BROWS, total_repeat_length=row_count)

    def evaluate(section, first, second):
        return evaluate_field(
            first, second, table, row_kind, kinds, bond_map, bond_strength, drive_amplitude[section]
        )

    new_real, new_imag = runge_kutta(real_part, imag_part, evaluate)
    return jnp.stack([new_real, new_imag])


def solution(mesh):
    in_specs = (P(None, ("grp", "dev"), None), P(), P(("grp", "dev")), P(), P(), P())
    out_specs = P(None, ("grp", "dev"), None)
    return jax.shard_map(body, mesh=mesh, in_specs=in_specs, out_specs=out_specs, check_vma=False)
```

profile of v0, /device:TPU:0, one launch (start us, length us, event | category | flops | bytes accessed | tf_op | source)
XLA Modules:
  0.0 155.7 jit_solution(2651413654822230415)
XLA Ops:
  0.9 3.0 %collective-permute-start.5 = (f32[64,128]{0,1:T(8,128)S(1)}, f32[64,128]{0,1:T(8,128)S(1)}, u32[]{:S(2)}, u32[]{:S(2)}) collective-permute-start(f32[64,128]{0,1:T(8,128)S(1)} %bitcast.508), channel_id=1, source_target_pairs={{0,1},{1,0},{2,3},{3,2},{4,5},{5,4},{6,7},{7,6},{8,9},{9,8},{10,11... | collective-permute-start | bytes 98312 | tf_op jit(solution)/shard_map/ppermute | solution.py:14
  3.9 1.6 %collective-permute-start.6 = (f32[64,128]{0,1:T(8,128)S(1)}, f32[64,128]{0,1:T(8,128)S(1)}, u32[]{:S(2)}, u32[]{:S(2)}) collective-permute-start(f32[64,128]{0,1:T(8,128)S(1)} %bitcast.509), channel_id=1, source_target_pairs={{0,2},{1,3},{2,0},{3,1},{4,6},{5,7},{6,4},{7,5},{8,10},{9,11},{10,... | collective-permute-start | bytes 98312 | tf_op jit(solution)/shard_map/ppermute | solution.py:14
  5.5 2.6 %collective-permute-start.7 = (f32[64,128]{0,1:T(8,128)S(1)}, f32[64,128]{0,1:T(8,128)S(1)}, u32[]{:S(2)}, u32[]{:S(2)}) collective-permute-start(f32[64,128]{0,1:T(8,128)S(1)} %bitcast.510), channel_id=1, source_target_pairs={{0,4},{1,5},{2,6},{3,7},{4,0},{5,1},{6,2},{7,3},{8,12},{9,13},{10,... | collective-permute-start | bytes 98312 | tf_op jit(solution)/shard_map/ppermute | solution.py:14
  8.1 1.5 collective-permute-start.9
  9.6 1.5 fusion.163
  15.0 1.5 fusion.159
  16.5 1.6 fusion.3
  19.4 2.5 %select_select_fusion = s32[64]{0:T(128)S(1)} fusion(pred[64]{0:T(512)(128)(4,1)S(1)} %copy-done.11, pred[64]{0:T(512)(128)(4,1)S(1)} %copy-done.12, pred[64]{0:T(512)(128)(4,1)S(1)} %copy-done.13, s32[]{:T(128)} %bitcast.11, s32[]{:T(128)} %bitcast.8, s32[]{:T(128)} %bitcast.9, s32[]{:T(128)} %bitcast.10), kind=kLoop, calls=%fused_computation.269 | loop fusion | flops 192 | bytes 464 | tf_op jit(solution)/shard_map/jit(_take)/gather | solution.py:118
  25.9 1.3 convert_multiply_fusion
  34.3 7.1 %multiply_add_fusion.4 = (f32[64,128]{0,1:T(8,128)}, f32[64,128]{0,1:T(8,128)}) fusion(f32[1,64,128]{1,2,0:T(8,128)S(1)} %copy.25, f32[64,128]{0,1:T(8,128)S(1)} %collective-permute-done.9, f32[]{:T(128)} %bitcast.31, f32[128,64]{1,0:T(8,128)S(1)} %gather_fusion.9, pred[128]{0:T(512)(128)(4,1)S(1)} %get-tuple-element.83, f32[128]{0:T(128)S(1)} %get-tuple-element.87, ...), kind=kLoop, calls=%fused_computation.250 | loop fusion | flops 311296 | bytes 494760 | tf_op jit(solution)/shard_map/add | solution.py:91
  41.4 1.8 %collective-permute-start.10 = (f32[64,128]{0,1:T(8,128)}, f32[64,128]{0,1:T(8,128)S(1)}, u32[]{:S(2)}, u32[]{:S(2)}) collective-permute-start(f32[64,128]{0,1:T(8,128)} %get-tuple-element.36), channel_id=1, source_target_pairs={{0,1},{1,0},{2,3},{3,2},{4,5},{5,4},{6,7},{7,6},{8,9},{9,8},{10,11... | collective-permute-start | bytes 98312 | tf_op jit(solution)/shard_map/ppermute | solution.py:14
  44.0 1.6 %collective-permute-start.11 = (f32[64,128]{0,1:T(8,128)}, f32[64,128]{0,1:T(8,128)S(1)}, u32[]{:S(2)}, u32[]{:S(2)}) collective-permute-start(f32[64,128]{0,1:T(8,128)} %get-tuple-element.36), channel_id=1, source_target_pairs={{0,2},{1,3},{2,0},{3,1},{4,6},{5,7},{6,4},{7,5},{8,10},{9,11},{10,... | collective-permute-start | bytes 98312 | tf_op jit(solution)/shard_map/ppermute | solution.py:14
  46.5 2.7 %collective-permute-start.12 = (f32[64,128]{0,1:T(8,128)}, f32[64,128]{0,1:T(8,128)S(1)}, u32[]{:S(2)}, u32[]{:S(2)}) collective-permute-start(f32[64,128]{0,1:T(8,128)} %get-tuple-element.36), channel_id=1, source_target_pairs={{0,4},{1,5},{2,6},{3,7},{4,0},{5,1},{6,2},{7,3},{8,12},{9,13},{10,... | collective-permute-start | bytes 98312 | tf_op jit(solution)/shard_map/ppermute | solution.py:14
  50.6 1.6 %collective-permute-start.14 = (f32[64,128]{0,1:T(8,128)}, f32[64,128]{0,1:T(8,128)S(1)}, u32[]{:S(2)}, u32[]{:S(2)}) collective-permute-start(f32[64,128]{0,1:T(8,128)} %get-tuple-element.36), channel_id=1, source_target_pairs={{0,16},{8,24},{16,0},{24,8},{1,17},{9,25},{17,1},{25,9},{2,18},{10... | collective-permute-start | bytes 98312 | tf_op jit(solution)/shard_map/ppermute | solution.py:14
  52.8 7.2 %multiply_add_fusion.5 = (f32[64,128]{0,1:T(8,128)}, f32[64,128]{0,1:T(8,128)}) fusion(f32[1,64,128]{1,2,0:T(8,128)S(1)} %copy.24, f32[64,128]{0,1:T(8,128)S(1)} %collective-permute-done.4, f32[]{:T(128)} %bitcast.31, f32[128,64]{1,0:T(8,128)S(1)} %gather_fusion.4, pred[128]{0:T(512)(128)(4,1)S(1)} %get-tuple-element.83, f32[128]{0:T(128)S(1)} %get-tuple-element.87, ...), kind=kLoop, calls=%fused_computation.251 | loop fusion | flops 303104 | bytes 494760 | tf_op jit(solution)/shard_map/add | solution.py:91
  60.0 2.4 %fusion.2 = f32[128,3072]{1,0:T(8,128)S(1)} fusion(f32[128,1536]{0,1:T(8,128)S(1)} %bitcast.505, f32[128,1536]{0,1:T(8,128)S(1)} %bitcast.501, f32[64,128]{0,1:T(8,128)} %get-tuple-element.36, f32[64,128]{0,1:T(8,128)} %get-tuple-element.34), kind=kOutput, calls=%fused_computation.43 | convolution fusion | flops 604389376 | bytes 3211264 | tf_op jit(solution)/shard_map/dot_general | solution.py:27
  68.6 8.0 %multiply_add_fusion.3 = (f32[64,128]{0,1:T(8,128)}, f32[64,128]{0,1:T(8,128)}) fusion(f32[1,64,128]{1,2,0:T(8,128)S(1)} %copy.24, f32[64,128]{0,1:T(8,128)S(1)} %collective-permute-done.14, f32[]{:T(128)} %bitcast.46, f32[128,64]{1,0:T(8,128)S(1)} %gather_fusion.14, pred[128]{0:T(512)(128)(4,1)S(1)} %get-tuple-element.83, f32[64,128]{0,1:T(8,128)} %get-tuple-element.36, ...), kind=kLoop, calls=%fused_computation.249 | loop fusion | flops 303104 | bytes 494760 | tf_op jit(solution)/shard_map/add | solution.py:94
  76.6 1.8 %collective-permute-start.25 = (f32[64,128]{0,1:T(8,128)}, f32[64,128]{0,1:T(8,128)S(1)}, u32[]{:S(2)}, u32[]{:S(2)}) collective-permute-start(f32[64,128]{0,1:T(8,128)} %get-tuple-element.30), channel_id=1, source_target_pairs={{0,1},{1,0},{2,3},{3,2},{4,5},{5,4},{6,7},{7,6},{8,9},{9,8},{10,11... | collective-permute-start | bytes 98312 | tf_op jit(solution)/shard_map/ppermute | solution.py:14
  79.2 1.6 %collective-permute-start.26 = (f32[64,128]{0,1:T(8,128)}, f32[64,128]{0,1:T(8,128)S(1)}, u32[]{:S(2)}, u32[]{:S(2)}) collective-permute-start(f32[64,128]{0,1:T(8,128)} %get-tuple-element.30), channel_id=1, source_target_pairs={{0,2},{1,3},{2,0},{3,1},{4,6},{5,7},{6,4},{7,5},{8,10},{9,11},{10,... | collective-permute-start | bytes 98312 | tf_op jit(solution)/shard_map/ppermute | solution.py:14
  81.6 2.7 %collective-permute-start.27 = (f32[64,128]{0,1:T(8,128)}, f32[64,128]{0,1:T(8,128)S(1)}, u32[]{:S(2)}, u32[]{:S(2)}) collective-permute-start(f32[64,128]{0,1:T(8,128)} %get-tuple-element.30), channel_id=1, source_target_pairs={{0,4},{1,5},{2,6},{3,7},{4,0},{5,1},{6,2},{7,3},{8,12},{9,13},{10,... | collective-permute-start | bytes 98312 | tf_op jit(solution)/shard_map/ppermute | solution.py:14
  85.8 1.6 collective-permute-start.29
  88.0 8.0 %multiply_add_fusion.2 = (f32[64,128]{0,1:T(8,128)}, f32[64,128]{0,1:T(8,128)}) fusion(f32[1,64,128]{1,2,0:T(8,128)S(1)} %copy.25, f32[64,128]{0,1:T(8,128)S(1)} %collective-permute-done.19, f32[]{:T(128)} %bitcast.46, f32[128,64]{1,0:T(8,128)S(1)} %gather_fusion.19, pred[128]{0:T(512)(128)(4,1)S(1)} %get-tuple-element.83, f32[64,128]{0,1:T(8,128)} %get-tuple-element.34, ...), kind=kLoop, calls=%fused_computation.248 | loop fusion | flops 311296 | bytes 494760 | tf_op jit(solution)/shard_map/add | solution.py:94
  96.0 2.4 %fusion.1 = f32[128,3072]{1,0:T(8,128)S(1)} fusion(f32[128,1536]{0,1:T(8,128)S(1)} %bitcast.506, f32[128,1536]{0,1:T(8,128)S(1)} %bitcast.502, f32[64,128]{0,1:T(8,128)} %get-tuple-element.32, f32[64,128]{0,1:T(8,128)} %get-tuple-element.30), kind=kOutput, calls=%fused_computation.42 | convolution fusion | flops 604389376 | bytes 3211264 | tf_op jit(solution)/shard_map/dot_general | solution.py:27
  104.8 7.2 %multiply_add_fusion = (f32[64,128]{0,1:T(8,128)S(1)}, f32[64,128]{0,1:T(8,128)S(1)}) fusion(f32[1,64,128]{1,2,0:T(8,128)S(1)} %copy.25, f32[64,128]{0,1:T(8,128)S(1)} %collective-permute-done.29, f32[]{:T(128)} %bitcast.61, f32[128,64]{1,0:T(8,128)S(1)} %gather_fusion.29, pred[128]{0:T(512)(128)(4,1)S(1)} %get-tuple-element.83, ...), kind=kLoop, calls=%fused_computation.246 | loop fusion | flops 311296 | bytes 494760 | tf_op jit(solution)/shard_map/add | solution.py:97
  112.0 1.9 %collective-permute-start.30 = (f32[64,128]{0,1:T(8,128)S(1)}, f32[64,128]{0,1:T(8,128)S(1)}, u32[]{:S(2)}, u32[]{:S(2)}) collective-permute-start(f32[64,128]{0,1:T(8,128)S(1)} %get-tuple-element.28), channel_id=1, source_target_pairs={{0,1},{1,0},{2,3},{3,2},{4,5},{5,4},{6,7},{7,6},{8,9},{9,8},{10,11... | collective-permute-start | bytes 98312 | tf_op jit(solution)/shard_map/ppermute | solution.py:14
  114.7 1.6 %collective-permute-start.31 = (f32[64,128]{0,1:T(8,128)S(1)}, f32[64,128]{0,1:T(8,128)S(1)}, u32[]{:S(2)}, u32[]{:S(2)}) collective-permute-start(f32[64,128]{0,1:T(8,128)S(1)} %get-tuple-element.28), channel_id=1, source_target_pairs={{0,2},{1,3},{2,0},{3,1},{4,6},{5,7},{6,4},{7,5},{8,10},{9,11},{10,... | collective-permute-start | bytes 98312 | tf_op jit(solution)/shard_map/ppermute | solution.py:14
  117.1 2.7 %collective-permute-start.32 = (f32[64,128]{0,1:T(8,128)S(1)}, f32[64,128]{0,1:T(8,128)S(1)}, u32[]{:S(2)}, u32[]{:S(2)}) collective-permute-start(f32[64,128]{0,1:T(8,128)S(1)} %get-tuple-element.28), channel_id=1, source_target_pairs={{0,4},{1,5},{2,6},{3,7},{4,0},{5,1},{6,2},{7,3},{8,12},{9,13},{10,... | collective-permute-start | bytes 98312 | tf_op jit(solution)/shard_map/ppermute | solution.py:14
  121.3 1.6 %collective-permute-start.34 = (f32[64,128]{0,1:T(8,128)S(1)}, f32[64,128]{0,1:T(8,128)S(1)}, u32[]{:S(2)}, u32[]{:S(2)}) collective-permute-start(f32[64,128]{0,1:T(8,128)S(1)} %get-tuple-element.28), channel_id=1, source_target_pairs={{0,16},{8,24},{16,0},{24,8},{1,17},{9,25},{17,1},{25,9},{2,18},{10... | collective-permute-start | bytes 98312 | tf_op jit(solution)/shard_map/ppermute | solution.py:14
  123.5 7.2 %multiply_add_fusion.1 = (f32[64,128]{0,1:T(8,128)S(1)}, f32[64,128]{0,1:T(8,128)S(1)}) fusion(f32[1,64,128]{1,2,0:T(8,128)S(1)} %copy.24, f32[64,128]{0,1:T(8,128)S(1)} %collective-permute-done.24, f32[]{:T(128)} %bitcast.61, f32[128,64]{1,0:T(8,128)S(1)} %gather_fusion.24, pred[128]{0:T(512)(128)(4,1)S(1)} %get-tuple-element.83, ...), kind=kLoop, calls=%fused_computation.247 | loop fusion | flops 303104 | bytes 494760 | tf_op jit(solution)/shard_map/add | solution.py:97
  130.7 1.6 fusion
  142.0 6.5 %fusion.42 = f32[1,64,128]{1,2,0:T(8,128)S(1)} fusion(f32[64,128]{0,1:T(8,128)S(1)} %copy.21, f32[128,64]{1,0:T(8,128)S(1)} %gather_fusion.34, f32[128,64]{1,0:T(8,128)S(1)} %gather_fusion.33, f32[128,64]{1,0:T(8,128)S(1)} %gather_fusion.32, f32[128,64]{1,0:T(8,128)S(1)} %gather_fusion.31, f32[128,64]{1,0:T(8,128)S(1)} %gather_fusion.30, ...), kind=kLoop, calls=%fused_computation.106 | loop fusion | flops 344064 | bytes 560296 | tf_op jit(solution)/shard_map/stack | solution.py:126
  148.5 6.5 %fusion.23 = f32[1,64,128]{1,2,0:T(8,128)S(1)} fusion(f32[64,128]{0,1:T(8,128)S(1)} %copy.22, f32[128,64]{1,0:T(8,128)S(1)} %gather_fusion.39, f32[128,64]{1,0:T(8,128)S(1)} %gather_fusion.38, f32[128,64]{1,0:T(8,128)S(1)} %gather_fusion.37, f32[128,64]{1,0:T(8,128)S(1)} %gather_fusion.36, f32[128,64]{1,0:T(8,128)S(1)} %gather_fusion.35, ...), kind=kLoop, calls=%fused_computation.82 | loop fusion | flops 352256 | bytes 560296 | tf_op jit(solution)/shard_map/stack | solution.py:126
  (181 shorter events, 47.6 us)
Async XLA Ops:
  0.9 28.2 %collective-permute-start.5 = (f32[64,128]{0,1:T(8,128)S(1)}, f32[64,128]{0,1:T(8,128)S(1)}, u32[]{:S(2)}, u32[]{:S(2)}) collective-permute-start(f32[64,128]{0,1:T(8,128)S(1)} %bitcast.508), channel_id=1, source_target_pairs={{0,1},{1,0},{2,3},{3,2},{4,5},{5,4},{6,7},{7,6},{8,9},{9,8},{10,11... | collective-permute-start | bytes 98312 | tf_op jit(solution)/shard_map/ppermute | solution.py:14
  3.9 26.3 %collective-permute-start.6 = (f32[64,128]{0,1:T(8,128)S(1)}, f32[64,128]{0,1:T(8,128)S(1)}, u32[]{:S(2)}, u32[]{:S(2)}) collective-permute-start(f32[64,128]{0,1:T(8,128)S(1)} %bitcast.509), channel_id=1, source_target_pairs={{0,2},{1,3},{2,0},{3,1},{4,6},{5,7},{6,4},{7,5},{8,10},{9,11},{10,... | collective-permute-start | bytes 98312 | tf_op jit(solution)/shard_map/ppermute | solution.py:14
  5.5 25.9 %collective-permute-start.7 = (f32[64,128]{0,1:T(8,128)S(1)}, f32[64,128]{0,1:T(8,128)S(1)}, u32[]{:S(2)}, u32[]{:S(2)}) collective-permute-start(f32[64,128]{0,1:T(8,128)S(1)} %bitcast.510), channel_id=1, source_target_pairs={{0,4},{1,5},{2,6},{3,7},{4,0},{5,1},{6,2},{7,3},{8,12},{9,13},{10,... | collective-permute-start | bytes 98312 | tf_op jit(solution)/shard_map/ppermute | solution.py:14
  8.1 24.4 %collective-permute-start.8 = (f32[64,128]{0,1:T(8,128)S(1)}, f32[64,128]{0,1:T(8,128)S(1)}, u32[]{:S(2)}, u32[]{:S(2)}) collective-permute-start(f32[64,128]{0,1:T(8,128)S(1)} %bitcast.511), channel_id=1, source_target_pairs={{0,8},{8,0},{16,24},{24,16},{1,9},{9,1},{17,25},{25,17},{2,10},{10... | collective-permute-start | bytes 98312 | tf_op jit(solution)/shard_map/ppermute | solution.py:14
  8.1 25.3 %collective-permute-start.9 = (f32[64,128]{0,1:T(8,128)S(1)}, f32[64,128]{0,1:T(8,128)S(1)}, u32[]{:S(2)}, u32[]{:S(2)}) collective-permute-start(f32[64,128]{0,1:T(8,128)S(1)} %bitcast.512), channel_id=1, source_target_pairs={{0,16},{8,24},{16,0},{24,8},{1,17},{9,25},{17,1},{25,9},{2,18},{10... | collective-permute-start | bytes 98312 | tf_op jit(solution)/shard_map/ppermute | solution.py:14
  30.3 13.8 %collective-permute-start.1 = (f32[64,128]{0,1:T(8,128)S(1)}, f32[64,128]{0,1:T(8,128)S(1)}, u32[]{:S(2)}, u32[]{:S(2)}) collective-permute-start(f32[64,128]{0,1:T(8,128)S(1)} %bitcast.516), channel_id=1, source_target_pairs={{0,2},{1,3},{2,0},{3,1},{4,6},{5,7},{6,4},{7,5},{8,10},{9,11},{10,... | collective-permute-start | bytes 98312 | tf_op jit(solution)/shard_map/ppermute | solution.py:14
  31.4 15.0 %collective-permute-start.2 = (f32[64,128]{0,1:T(8,128)S(1)}, f32[64,128]{0,1:T(8,128)S(1)}, u32[]{:S(2)}, u32[]{:S(2)}) collective-permute-start(f32[64,128]{0,1:T(8,128)S(1)} %bitcast.517), channel_id=1, source_target_pairs={{0,4},{1,5},{2,6},{3,7},{4,0},{5,1},{6,2},{7,3},{8,12},{9,13},{10,... | collective-permute-start | bytes 98312 | tf_op jit(solution)/shard_map/ppermute | solution.py:14
  32.5 17.4 %collective-permute-start.3 = (f32[64,128]{0,1:T(8,128)S(1)}, f32[64,128]{0,1:T(8,128)S(1)}, u32[]{:S(2)}, u32[]{:S(2)}) collective-permute-start(f32[64,128]{0,1:T(8,128)S(1)} %bitcast.518), channel_id=1, source_target_pairs={{0,8},{8,0},{16,24},{24,16},{1,9},{9,1},{17,25},{25,17},{2,10},{10... | collective-permute-start | bytes 98312 | tf_op jit(solution)/shard_map/ppermute | solution.py:14
  33.4 17.3 %collective-permute-start.4 = (f32[64,128]{0,1:T(8,128)S(1)}, f32[64,128]{0,1:T(8,128)S(1)}, u32[]{:S(2)}, u32[]{:S(2)}) collective-permute-start(f32[64,128]{0,1:T(8,128)S(1)} %bitcast.519), channel_id=1, source_target_pairs={{0,16},{8,24},{16,0},{24,8},{1,17},{9,25},{17,1},{25,9},{2,18},{10... | collective-permute-start | bytes 98312 | tf_op jit(solution)/shard_map/ppermute | solution.py:14
  41.4 21.7 %collective-permute-start.10 = (f32[64,128]{0,1:T(8,128)}, f32[64,128]{0,1:T(8,128)S(1)}, u32[]{:S(2)}, u32[]{:S(2)}) collective-permute-start(f32[64,128]{0,1:T(8,128)} %get-tuple-element.36), channel_id=1, source_target_pairs={{0,1},{1,0},{2,3},{3,2},{4,5},{5,4},{6,7},{7,6},{8,9},{9,8},{10,11... | collective-permute-start | bytes 98312 | tf_op jit(solution)/shard_map/ppermute | solution.py:14
  44.0 20.5 %collective-permute-start.11 = (f32[64,128]{0,1:T(8,128)}, f32[64,128]{0,1:T(8,128)S(1)}, u32[]{:S(2)}, u32[]{:S(2)}) collective-permute-start(f32[64,128]{0,1:T(8,128)} %get-tuple-element.36), channel_id=1, source_target_pairs={{0,2},{1,3},{2,0},{3,1},{4,6},{5,7},{6,4},{7,5},{8,10},{9,11},{10,... | collective-permute-start | bytes 98312 | tf_op jit(solution)/shard_map/ppermute | solution.py:14
  46.5 19.4 %collective-permute-start.12 = (f32[64,128]{0,1:T(8,128)}, f32[64,128]{0,1:T(8,128)S(1)}, u32[]{:S(2)}, u32[]{:S(2)}) collective-permute-start(f32[64,128]{0,1:T(8,128)} %get-tuple-element.36), channel_id=1, source_target_pairs={{0,4},{1,5},{2,6},{3,7},{4,0},{5,1},{6,2},{7,3},{8,12},{9,13},{10,... | collective-permute-start | bytes 98312 | tf_op jit(solution)/shard_map/ppermute | solution.py:14
  49.9 17.1 %collective-permute-start.13 = (f32[64,128]{0,1:T(8,128)}, f32[64,128]{0,1:T(8,128)S(1)}, u32[]{:S(2)}, u32[]{:S(2)}) collective-permute-start(f32[64,128]{0,1:T(8,128)} %get-tuple-element.36), channel_id=1, source_target_pairs={{0,8},{8,0},{16,24},{24,16},{1,9},{9,1},{17,25},{25,17},{2,10},{10... | collective-permute-start | bytes 98312 | tf_op jit(solution)/shard_map/ppermute | solution.py:14
  50.6 17.1 %collective-permute-start.14 = (f32[64,128]{0,1:T(8,128)}, f32[64,128]{0,1:T(8,128)S(1)}, u32[]{:S(2)}, u32[]{:S(2)}) collective-permute-start(f32[64,128]{0,1:T(8,128)} %get-tuple-element.36), channel_id=1, source_target_pairs={{0,16},{8,24},{16,0},{24,8},{1,17},{9,25},{17,1},{25,9},{2,18},{10... | collective-permute-start | bytes 98312 | tf_op jit(solution)/shard_map/ppermute | solution.py:14
  63.2 13.4 %collective-permute-start.15 = (f32[64,128]{0,1:T(8,128)}, f32[64,128]{0,1:T(8,128)S(1)}, u32[]{:S(2)}, u32[]{:S(2)}) collective-permute-start(f32[64,128]{0,1:T(8,128)} %get-tuple-element.34), channel_id=1, source_target_pairs={{0,1},{1,0},{2,3},{3,2},{4,5},{5,4},{6,7},{7,6},{8,9},{9,8},{10,11... | collective-permute-start | bytes 98312 | tf_op jit(solution)/shard_map/ppermute | solution.py:14
  64.5 14.7 %collective-permute-start.16 = (f32[64,128]{0,1:T(8,128)}, f32[64,128]{0,1:T(8,128)S(1)}, u32[]{:S(2)}, u32[]{:S(2)}) collective-permute-start(f32[64,128]{0,1:T(8,128)} %get-tuple-element.34), channel_id=1, source_target_pairs={{0,2},{1,3},{2,0},{3,1},{4,6},{5,7},{6,4},{7,5},{8,10},{9,11},{10,... | collective-permute-start | bytes 98312 | tf_op jit(solution)/shard_map/ppermute | solution.py:14
  65.8 15.8 %collective-permute-start.17 = (f32[64,128]{0,1:T(8,128)}, f32[64,128]{0,1:T(8,128)S(1)}, u32[]{:S(2)}, u32[]{:S(2)}) collective-permute-start(f32[64,128]{0,1:T(8,128)} %get-tuple-element.34), channel_id=1, source_target_pairs={{0,4},{1,5},{2,6},{3,7},{4,0},{5,1},{6,2},{7,3},{8,12},{9,13},{10,... | collective-permute-start | bytes 98312 | tf_op jit(solution)/shard_map/ppermute | solution.py:14
  67.0 18.1 %collective-permute-start.18 = (f32[64,128]{0,1:T(8,128)}, f32[64,128]{0,1:T(8,128)S(1)}, u32[]{:S(2)}, u32[]{:S(2)}) collective-permute-start(f32[64,128]{0,1:T(8,128)} %get-tuple-element.34), channel_id=1, source_target_pairs={{0,8},{8,0},{16,24},{24,16},{1,9},{9,1},{17,25},{25,17},{2,10},{10... | collective-permute-start | bytes 98312 | tf_op jit(solution)/shard_map/ppermute | solution.py:14
  67.7 18.1 %collective-permute-start.19 = (f32[64,128]{0,1:T(8,128)}, f32[64,128]{0,1:T(8,128)S(1)}, u32[]{:S(2)}, u32[]{:S(2)}) collective-permute-start(f32[64,128]{0,1:T(8,128)} %get-tuple-element.34), channel_id=1, source_target_pairs={{0,16},{8,24},{16,0},{24,8},{1,17},{9,25},{17,1},{25,9},{2,18},{10... | collective-permute-start | bytes 98312 | tf_op jit(solution)/shard_map/ppermute | solution.py:14
  76.6 22.8 %collective-permute-start.25 = (f32[64,128]{0,1:T(8,128)}, f32[64,128]{0,1:T(8,128)S(1)}, u32[]{:S(2)}, u32[]{:S(2)}) collective-permute-start(f32[64,128]{0,1:T(8,128)} %get-tuple-element.30), channel_id=1, source_target_pairs={{0,1},{1,0},{2,3},{3,2},{4,5},{5,4},{6,7},{7,6},{8,9},{9,8},{10,11... | collective-permute-start | bytes 98312 | tf_op jit(solution)/shard_map/ppermute | solution.py:14
  79.2 21.5 %collective-permute-start.26 = (f32[64,128]{0,1:T(8,128)}, f32[64,128]{0,1:T(8,128)S(1)}, u32[]{:S(2)}, u32[]{:S(2)}) collective-permute-start(f32[64,128]{0,1:T(8,128)} %get-tuple-element.30), channel_id=1, source_target_pairs={{0,2},{1,3},{2,0},{3,1},{4,6},{5,7},{6,4},{7,5},{8,10},{9,11},{10,... | collective-permute-start | bytes 98312 | tf_op jit(solution)/shard_map/ppermute | solution.py:14
  81.6 20.4 %collective-permute-start.27 = (f32[64,128]{0,1:T(8,128)}, f32[64,128]{0,1:T(8,128)S(1)}, u32[]{:S(2)}, u32[]{:S(2)}) collective-permute-start(f32[64,128]{0,1:T(8,128)} %get-tuple-element.30), channel_id=1, source_target_pairs={{0,4},{1,5},{2,6},{3,7},{4,0},{5,1},{6,2},{7,3},{8,12},{9,13},{10,... | collective-permute-start | bytes 98312 | tf_op jit(solution)/shard_map/ppermute | solution.py:14
  85.1 18.1 %collective-permute-start.28 = (f32[64,128]{0,1:T(8,128)}, f32[64,128]{0,1:T(8,128)S(1)}, u32[]{:S(2)}, u32[]{:S(2)}) collective-permute-start(f32[64,128]{0,1:T(8,128)} %get-tuple-element.30), channel_id=1, source_target_pairs={{0,8},{8,0},{16,24},{24,16},{1,9},{9,1},{17,25},{25,17},{2,10},{10... | collective-permute-start | bytes 98312 | tf_op jit(solution)/shard_map/ppermute | solution.py:14
  85.8 18.1 %collective-permute-start.29 = (f32[64,128]{0,1:T(8,128)}, f32[64,128]{0,1:T(8,128)S(1)}, u32[]{:S(2)}, u32[]{:S(2)}) collective-permute-start(f32[64,128]{0,1:T(8,128)} %get-tuple-element.30), channel_id=1, source_target_pairs={{0,16},{8,24},{16,0},{24,8},{1,17},{9,25},{17,1},{25,9},{2,18},{10... | collective-permute-start | bytes 98312 | tf_op jit(solution)/shard_map/ppermute | solution.py:14
  100.7 14.0 %collective-permute-start.21 = (f32[64,128]{0,1:T(8,128)}, f32[64,128]{0,1:T(8,128)S(1)}, u32[]{:S(2)}, u32[]{:S(2)}) collective-permute-start(f32[64,128]{0,1:T(8,128)} %get-tuple-element.32), channel_id=1, source_target_pairs={{0,2},{1,3},{2,0},{3,1},{4,6},{5,7},{6,4},{7,5},{8,10},{9,11},{10,... | collective-permute-start | bytes 98312 | tf_op jit(solution)/shard_map/ppermute | solution.py:14
  102.0 15.1 %collective-permute-start.22 = (f32[64,128]{0,1:T(8,128)}, f32[64,128]{0,1:T(8,128)S(1)}, u32[]{:S(2)}, u32[]{:S(2)}) collective-permute-start(f32[64,128]{0,1:T(8,128)} %get-tuple-element.32), channel_id=1, source_target_pairs={{0,4},{1,5},{2,6},{3,7},{4,0},{5,1},{6,2},{7,3},{8,12},{9,13},{10,... | collective-permute-start | bytes 98312 | tf_op jit(solution)/shard_map/ppermute | solution.py:14
  103.2 17.4 %collective-permute-start.23 = (f32[64,128]{0,1:T(8,128)}, f32[64,128]{0,1:T(8,128)S(1)}, u32[]{:S(2)}, u32[]{:S(2)}) collective-permute-start(f32[64,128]{0,1:T(8,128)} %get-tuple-element.32), channel_id=1, source_target_pairs={{0,8},{8,0},{16,24},{24,16},{1,9},{9,1},{17,25},{25,17},{2,10},{10... | collective-permute-start | bytes 98312 | tf_op jit(solution)/shard_map/ppermute | solution.py:14
  103.9 17.4 %collective-permute-start.24 = (f32[64,128]{0,1:T(8,128)}, f32[64,128]{0,1:T(8,128)S(1)}, u32[]{:S(2)}, u32[]{:S(2)}) collective-permute-start(f32[64,128]{0,1:T(8,128)} %get-tuple-element.32), channel_id=1, source_target_pairs={{0,16},{8,24},{16,0},{24,8},{1,17},{9,25},{17,1},{25,9},{2,18},{10... | collective-permute-start | bytes 98312 | tf_op jit(solution)/shard_map/ppermute | solution.py:14
  112.0 20.4 %collective-permute-start.30 = (f32[64,128]{0,1:T(8,128)S(1)}, f32[64,128]{0,1:T(8,128)S(1)}, u32[]{:S(2)}, u32[]{:S(2)}) collective-permute-start(f32[64,128]{0,1:T(8,128)S(1)} %get-tuple-element.28), channel_id=1, source_target_pairs={{0,1},{1,0},{2,3},{3,2},{4,5},{5,4},{6,7},{7,6},{8,9},{9,8},{10,11... | collective-permute-start | bytes 98312 | tf_op jit(solution)/shard_map/ppermute | solution.py:14
  114.7 18.3 %collective-permute-start.31 = (f32[64,128]{0,1:T(8,128)S(1)}, f32[64,128]{0,1:T(8,128)S(1)}, u32[]{:S(2)}, u32[]{:S(2)}) collective-permute-start(f32[64,128]{0,1:T(8,128)S(1)} %get-tuple-element.28), channel_id=1, source_target_pairs={{0,2},{1,3},{2,0},{3,1},{4,6},{5,7},{6,4},{7,5},{8,10},{9,11},{10,... | collective-permute-start | bytes 98312 | tf_op jit(solution)/shard_map/ppermute | solution.py:14
  117.1 16.4 %collective-permute-start.32 = (f32[64,128]{0,1:T(8,128)S(1)}, f32[64,128]{0,1:T(8,128)S(1)}, u32[]{:S(2)}, u32[]{:S(2)}) collective-permute-start(f32[64,128]{0,1:T(8,128)S(1)} %get-tuple-element.28), channel_id=1, source_target_pairs={{0,4},{1,5},{2,6},{3,7},{4,0},{5,1},{6,2},{7,3},{8,12},{9,13},{10,... | collective-permute-start | bytes 98312 | tf_op jit(solution)/shard_map/ppermute | solution.py:14
  120.5 13.3 %collective-permute-start.33 = (f32[64,128]{0,1:T(8,128)S(1)}, f32[64,128]{0,1:T(8,128)S(1)}, u32[]{:S(2)}, u32[]{:S(2)}) collective-permute-start(f32[64,128]{0,1:T(8,128)S(1)} %get-tuple-element.28), channel_id=1, source_target_pairs={{0,8},{8,0},{16,24},{24,16},{1,9},{9,1},{17,25},{25,17},{2,10},{10... | collective-permute-start | bytes 98312 | tf_op jit(solution)/shard_map/ppermute | solution.py:14
  (22 other events, 172.7 us)
where the time goes:
time: 157 us; the launch traced here: 156 us
  other arithmetic  67 us (43%)
  starting transfers between devices  39.3 us (25%)
  local copies, waits for them, and re-layouts  37.5 us (24%)
  matrix products  7.94 us (5%)
  between operations  3.95 us (3%)
    ppermute x40, starting transfers between devices, swapped(): lax.ppermute(shard, axis, [(i, i ^ 1 << distance) for i in range(lax.axis...  39.3 us
    gather x20, local copies, waits for them, and re-layouts, evaluate_field(): jnp.take(part_imag, shuffle, axis=1)  14.3 us
    gather x20, local copies, waits for them, and re-layouts, evaluate_field(): jnp.take(part_real, shuffle, axis=1)  14.1 us
    another operation x3, other arithmetic, body(): return jnp.stack([new_real, new_imag])  13 us
    add x1, other arithmetic, runge_kutta(): imag_part + half_step * slope_two[1]  8 us
    add x1, other arithmetic, runge_kutta(): real_part + half_step * slope_two[0]  7.98 us
    dot_general x4, matrix products, coupled(): jnp.dot(jnp.concatenate([real_part, imag_part], 0), table, precision=HIGH...  7.94 us
    add x1, other arithmetic, runge_kutta(): imag_part + STEP_SIZE * slope_three[1]  7.17 us
  transfers between devices with their start and end apart: 40, of which 0 were waited for; matrix products, arithmetic and copies ran while one was open for 62% of the time, Pallas kernels for 0%

commit v1 on v0

--- a/solution.py
+++ b/solution.py
@@ -1,6 +1,10 @@
+import functools
+
 import jax
 import jax.numpy as jnp
 from jax import lax
+from jax.experimental import pallas as pl
+from jax.experimental.pallas import tpu as pltpu
 from jax.sharding import PartitionSpec as P
 
 BROWS = 16
@@ -126,7 +130,251 @@
     return jnp.stack([new_real, new_imag])
 
 
+SUBLANES = 8
+MESH = pl.DeviceIdType.MESH
+
+
+def flipped(field, stride):
+    row_count, col_count = field.shape
+    if stride >= SUBLANES:
+        folded = field.reshape(row_count // (2 * stride), 2, stride, col_count)
+        return jnp.concatenate([folded[:, 1:], folded[:, :1]], 1).reshape(row_count, col_count)
+    tiles = field.reshape(row_count // SUBLANES, SUBLANES, col_count)
+    down = pltpu.roll(tiles, stride, 1)
+    if 2 * stride < SUBLANES:
+        row = lax.broadcasted_iota(jnp.int32, tiles.shape, 1)
+        up = pltpu.roll(tiles, SUBLANES - stride, 1)
+        down = jnp.where(row // stride % 2 == 1, down, up)
+    return down.reshape(row_count, col_count)
+
+
+def step_kernel(
+    sizes,
+    kind_ref,
+    bond_ref,
+    strength_ref,
+    drive_ref,
+    amp_ref,
+    coup_ref,
+    out_ref,
+    stage,
+    held,
+    table,
+    weight_high,
+    weight_low,
+    masks,
+    diagonal,
+    field,
+    total,
+    final,
+    local_sem,
+    send_sem,
+    recv_sem,
+):
+    grp_size, dev_size, block_rows = sizes
+    devices = grp_size * dev_size
+    lead = spin_count(devices)
+    row_count, col_count = amp_ref.shape[1:]
+    kinds = coup_ref.shape[1]
+    sections = drive_ref.shape[0]
+    share = row_count // devices
+    others = (devices - 1) * share
+    me = lax.axis_index("grp") * dev_size + lax.axis_index("dev")
+
+    def place(hop):
+        other = lax.rem(me + hop, devices)
+        return other, (other // dev_size, lax.rem(other, dev_size))
+
+    load_table = pltpu.make_async_copy(coup_ref, table, local_sem.at[0])
+    load_table.start()
+    barrier = pltpu.get_barrier_semaphore()
+
+    def greet(hop, carry):
+        pl.semaphore_signal(barrier, inc=1, device_id=place(hop)[1], device_id_type=MESH)
+        return carry
+
+    lax.fori_loop(1, devices, greet, 0)
+    stage[0] = amp_ref[0]
+    stage[1] = amp_ref[1]
+    for block in range(row_count // block_rows):
+        kind = kind_ref[block].astype(jnp.float32)
+        stage[2, block * block_rows : (block + 1) * block_rows] = jnp.full(
+            (block_rows, col_count), kind, jnp.float32
+        )
+    pl.semaphore_wait(barrier, devices - 1)
+
+    mine = pl.ds(me * share, share)
+
+    def exchange(source, target, phase):
+        def send(hop, carry):
+            other, where = place(hop)
+            pltpu.make_async_remote_copy(
+                src_ref=source.at[:, pl.ds(other * share, share)],
+                dst_ref=target.at[:, mine],
+                send_sem=send_sem.at[phase],
+                recv_sem=recv_sem.at[phase],
+                device_id=where,
+                device_id_type=MESH,
+            ).start()
+            return carry
+
+        lax.fori_loop(1, devices, send, 0)
+        own = pltpu.make_async_copy(
+            source.at[:, mine], target.at[:, mine], local_sem.at[1 + phase]
+        )
+        own.start()
+        return own
+
+    def finish(source, target, phase, own):
+        own.wait()
+        sent = source.at[:, pl.ds(0, others)]
+        pltpu.make_async_copy(sent, sent, send_sem.at[phase]).wait()
+        came = target.at[:, pl.ds(0, others)]
+        pltpu.make_async_copy(came, came, recv_sem.at[phase]).wait()
+
+    own = exchange(stage, held, 0)
+    load_table.wait()
+
+    def split(kind, carry):
+        real = table[0, kind]
+        imag = table[1, kind]
+        real_high = real.astype(jnp.bfloat16)
+        imag_high = imag.astype(jnp.bfloat16)
+        real_low = (real - real_high.astype(jnp.float32)).astype(jnp.bfloat16)
+        imag_low = (imag - imag_high.astype(jnp.float32)).astype(jnp.bfloat16)
+        first = pl.ds(pl.multiple_of(kind * 2 * col_count, 2 * col_count), col_count)
+        second = pl.ds(pl.multiple_of(kind * 2 * col_count, col_count) + col_count, col_count)
+        for weight, real_now, imag_now in (
+            (weight_high, real_high, imag_high),
+            (weight_low, real_low, imag_low),
+        ):
+            weight[first, :col_count] = -imag_now
+            weight[first, col_count:] = -real_now
+            weight[second, :col_count] = real_now
+            weight[second, col_count:] = -imag_now
+        return carry
+
+    lax.fori_loop(0, kinds, split, 0)
+
+    row = lax.broadcasted_iota(jnp.int32, (row_count, col_count), 0)
+    column = lax.broadcasted_iota(jnp.int32, (row_count, col_count), 1)
+    diag = jnp.zeros((row_count, col_count), jnp.float32)
+    shuffles = []
+    for spin in range(lead):
+        target = bond_ref[spin]
+        shuffles.append(jnp.bitwise_xor(column, jnp.left_shift(jnp.int32(1), target)))
+        parity = jnp.bitwise_xor(
+            jnp.right_shift(row // share, spin), jnp.right_shift(column, target)
+        )
+        sign = (1 - 2 * jnp.bitwise_and(parity, 1)).astype(jnp.float32)
+        diag = diag + strength_ref[spin] * sign
+    diagonal[...] = diag
+
+    finish(stage, held, 0, own)
+    kind_rows = held[2]
+    for kind in range(kinds):
+        masks[kind] = (kind_rows == float(kind)).astype(jnp.float32).astype(jnp.bfloat16)
+    field[...] = held[:2]
+    total[...] = jnp.zeros_like(total)
+
+    def section(now, carry):
+        both = jnp.concatenate([field[0], field[1]], 1)
+        high = both.astype(jnp.bfloat16)
+        low = (both - high.astype(jnp.float32)).astype(jnp.bfloat16)
+        high_parts = []
+        low_parts = []
+        for kind in range(kinds):
+            mask = jnp.concatenate([masks[kind], masks[kind]], 1)
+            high_parts.append(high * mask)
+            low_parts.append(low * mask)
+        high_all = jnp.concatenate(high_parts, 1)
+        low_all = jnp.concatenate(low_parts, 1)
+        main = jnp.dot(
+            jnp.concatenate([high_all, low_all], 0),
+            weight_high[...],
+            preferred_element_type=jnp.float32,
+        )
+        rest = jnp.dot(high_all, weight_low[...], preferred_element_type=jnp.float32)
+        product = main[:row_count] + (main[row_count:] + rest)
+        leads = []
+        for part in range(2):
+            here = field[part]
+            other = diagonal[...] * here
+            for spin in range(lead):
+                there = flipped(here, share << spin)
+                moved = jnp.take_along_axis(
+                    there, shuffles[spin], axis=1, mode="promise_in_bounds"
+                )
+                other = other + strength_ref[spin] * moved + drive_ref[now, spin] * there
+            leads.append(other)
+        slope = (product[:, :col_count] + leads[1], product[:, col_count:] - leads[0])
+        edge = (now == 0) | (now == sections - 1)
+        weight = jnp.where(edge, 1.0, 2.0)
+        step = jnp.where(now == sections - 2, STEP_SIZE, 0.5 * STEP_SIZE)
+        for part in range(2):
+            total[part] = total[part] + weight * slope[part]
+            field[part] = held[part] + step * slope[part]
+        return carry
+
+    lax.fori_loop(0, sections, section, 0)
+    final[...] = held[:2] + (STEP_SIZE / 6.0) * total[...]
+    own = exchange(final, out_ref, 1)
+    finish(final, out_ref, 1, own)
+
+
+def body_by_rows(
+    sizes, amplitudes, couplings, block_index, bond_map, bond_strength, drive_amplitude
+):
+    parts, row_count, col_count = amplitudes.shape
+    kinds = couplings.shape[1]
+    block_rows = row_count // block_index.shape[0]
+    half = (parts, row_count, col_count)
+    smem = pl.BlockSpec(memory_space=pltpu.SMEM)
+    vmem = pl.BlockSpec(memory_space=pltpu.VMEM)
+    weight = pltpu.VMEM((kinds * 2 * col_count, 2 * col_count), jnp.bfloat16)
+    return pl.pallas_call(
+        functools.partial(step_kernel, (*sizes, block_rows)),
+        out_shape=jax.ShapeDtypeStruct(half, jnp.float32),
+        in_specs=[smem, smem, smem, smem, vmem, pl.BlockSpec(memory_space=pl.ANY)],
+        out_specs=vmem,
+        scratch_shapes=[
+            pltpu.VMEM((parts + 1, row_count, col_count), jnp.float32),
+            pltpu.VMEM((parts + 1, row_count, col_count), jnp.float32),
+            pltpu.VMEM(couplings.shape, jnp.float32),
+            weight,
+            weight,
+            pltpu.VMEM((kinds, row_count, col_count), jnp.bfloat16),
+            pltpu.VMEM((row_count, col_count), jnp.float32),
+            pltpu.VMEM(half, jnp.float32),
+            pltpu.VMEM(half, jnp.float32),
+            pltpu.VMEM(half, jnp.float32),
+            pltpu.SemaphoreType.DMA((3,)),
+            pltpu.SemaphoreType.DMA((2,)),
+            pltpu.SemaphoreType.DMA((2,)),
+        ],
+        compiler_params=pltpu.CompilerParams(
+            collective_id=0, has_side_effects=True, vmem_limit_bytes=32 * 2**20
+        ),
+    )(block_index, bond_map, bond_strength, drive_amplitude, amplitudes, couplings)
+
+
+def chosen_body(sizes, amplitudes, couplings, block_index, *rest):
+    row_count = amplitudes.shape[1]
+    devices = sizes[0] * sizes[1]
+    block_rows = row_count // block_index.shape[0]
+    if row_count % devices == 0 and block_rows % (row_count // devices) == 0:
+        return body_by_rows(sizes, amplitudes, couplings, block_index, *rest)
+    return body(amplitudes, couplings, block_index, *rest)
+
+
 def solution(mesh):
     in_specs = (P(None, ("grp", "dev"), None), P(), P(("grp", "dev")), P(), P(), P())
     out_specs = P(None, ("grp", "dev"), None)
-    return jax.shard_map(body, mesh=mesh, in_specs=in_specs, out_specs=out_specs, check_vma=False)
+    sizes = (mesh.shape["grp"], mesh.shape["dev"])
+    return jax.shard_map(
+        functools.partial(chosen_body, sizes),
+        mesh=mesh,
+        in_specs=in_specs,
+        out_specs=out_specs,
+        check_vma=False,
+    )

time: 157 us -> 26.1 us (0.17)
  other arithmetic: 67 us -> 0 us
  starting transfers between devices: 39.3 us -> 0 us
  local copies, waits for them, and re-layouts: 37.5 us -> 5.52 us
  Pallas kernels: 0 us -> 20.3 us
  matrix products: 7.94 us -> 0 us
  between operations: 3.95 us -> 0.02 us
    add x6 -> x0, other arithmetic: 44.6 us -> none  [the longest x1 8 us: runge_kutta(): imag_part + half_step * slope_two[1]]
    ppermute x40 -> x0, starting transfers between devices: 39.3 us -> none  [swapped(): lax.ppermute(shard, axis, [(i, i ^ 1 << distance) for i in range(lax.axis...]
    gather x41 -> x0, local copies, waits for them, and re-layouts: 29.1 us -> none  [the longest x20 14.3 us: evaluate_field(): jnp.take(part_imag, shuffle, axis=1)]
    pallas_call x0 -> x1, Pallas kernels: none -> 20.3 us  [body_by_rows(): pl.pallas_call(functools.partial(step_kernel, (*sizes, block_rows)), out_...]
    another operation x3 -> x0, other arithmetic: 13 us -> none  [body(): return jnp.stack([new_real, new_imag])]
    dot_general x4 -> x0, matrix products: 7.94 us -> none  [coupled(): jnp.dot(jnp.concatenate([real_part, imag_part], 0), table, precision=HIGH...]
    slice x6 -> x0, local copies, waits for them, and re-layouts: 5.77 us -> none  [the longest x1 1.49 us: evaluate_field(): target = bond_map[lead_spin]]
    unnamed x30 -> x13, local copies, waits for them, and re-layouts: 0.58 us -> 5.52 us
  transfers between devices with their start and end apart: 40 -> 0, of which waited for: 0 -> 0; matrix products, arithmetic and copies ran while one was open for 62% -> 0% of each run, Pallas kernels for 0% -> 0%
where the time goes in v1:
time: 26.1 us; the launch traced here: 25.9 us
  Pallas kernels  20.3 us (78%)
  local copies, waits for them, and re-layouts  5.52 us (21%)
    pallas_call x1, Pallas kernels, body_by_rows(): pl.pallas_call(functools.partial(step_kernel, (*sizes, block_rows)), out_...  20.3 us
    unnamed x13, local copies, waits for them, and re-layouts  5.52 us

profile of v1, /device:TPU:0, one launch (start us, length us, event | category | flops | bytes accessed | tf_op | source)
XLA Modules:
  0.0 25.9 jit_solution(4568645855291431089)
XLA Ops:
  0.0 0.0 copy-start
  0.0 1.4 %copy-done = f32[2,12,128,128]{3,2,1,0:T(8,128)S(1)} copy-done((f32[2,12,128,128]{3,2,1,0:T(8,128)S(1)}, f32[2,12,128,128]{3,2,1,0:T(8,128)}, u32[]{:S(2)}) %copy-start) | copy-done | bytes 1572888
  1.4 0.0 copy-start.1
  1.4 0.8 %copy-done.1 = f32[2,64,128]{2,1,0:T(8,128)S(1)} copy-done((f32[2,64,128]{2,1,0:T(8,128)S(1)}, f32[2,64,128]{2,1,0:T(8,128)}, u32[]{:S(2)}) %copy-start.1) | copy-done | bytes 65560
  2.2 0.0 copy-start.2
  2.3 0.7 %copy-done.2 = f32[4,5]{1,0:T(4,128)S(1)} copy-done((f32[4,5]{1,0:T(4,128)S(1)}, f32[4,5]{1,0:T(4,128)}, u32[]{:S(2)}) %copy-start.2) | copy-done | bytes 104
  2.9 0.0 copy-start.3
  2.9 0.7 %copy-done.3 = s32[4]{0:T(128)S(1)} copy-done((s32[4]{0:T(128)S(1)}, s32[4]{0:T(128)}, u32[]{:S(2)}) %copy-start.3) | copy-done | bytes 40
  3.6 0.0 copy-start.4
  3.6 0.7 %copy-done.4 = s32[5]{0:T(128)S(1)} copy-done((s32[5]{0:T(128)S(1)}, s32[5]{0:T(128)}, u32[]{:S(2)}) %copy-start.4) | copy-done | bytes 44
  4.2 0.0 copy-start.5
  4.2 0.7 %copy-done.5 = f32[5]{0:T(128)S(1)} copy-done((f32[5]{0:T(128)S(1)}, f32[5]{0:T(128)}, u32[]{:S(2)}) %copy-start.5) | copy-done | bytes 44
  4.9 20.3 %shard_map.64 = f32[2,64,128]{2,1,0:T(8,128)S(1)} custom-call(s32[4]{0:T(128)S(1)} %copy-done.3, s32[5]{0:T(128)S(1)} %copy-done.4, f32[5]{0:T(128)S(1)} %copy-done.5, f32[4,5]{1,0:T(4,128)S(1)} %copy-done.2, f32[2,64,128]{2,1,0:T(8,128)S(1)} %copy-done.1, f32[2,12,128,128]{3,2,1,0:T(8,128)S(1)} %copy-done), custom_call_target="tpu_custom_call" | custom-call | tf_op jit(solution)/shard_map/pallas_call | solution.py:335
  25.2 0.6 %copy.8 = f32[2,64,128]{2,1,0:T(8,128)} copy(f32[2,64,128]{2,1,0:T(8,128)S(1)} %shard_map.64) | data formatting | bytes 131072
Async XLA Ops:
  0.0 1.4 %copy-start = (f32[2,12,128,128]{3,2,1,0:T(8,128)S(1)}, f32[2,12,128,128]{3,2,1,0:T(8,128)}, u32[]{:S(2)}) copy-start(f32[2,12,128,128]{3,2,1,0:T(8,128)} %coup_ref.1) | copy-start | bytes 4718596
  1.4 0.8 %copy-start.1 = (f32[2,64,128]{2,1,0:T(8,128)S(1)}, f32[2,64,128]{2,1,0:T(8,128)}, u32[]{:S(2)}) copy-start(f32[2,64,128]{2,1,0:T(8,128)} %amp_ref.1) | copy-start | bytes 196612
  2.2 0.7 %copy-start.2 = (f32[4,5]{1,0:T(4,128)S(1)}, f32[4,5]{1,0:T(4,128)}, u32[]{:S(2)}) copy-start(f32[4,5]{1,0:T(4,128)} %drive_ref.1) | copy-start | bytes 244
  2.9 0.7 %copy-start.3 = (s32[4]{0:T(128)S(1)}, s32[4]{0:T(128)}, u32[]{:S(2)}) copy-start(s32[4]{0:T(128)} %kind_ref.1) | copy-start | bytes 52
  3.6 0.7 %copy-start.4 = (s32[5]{0:T(128)S(1)}, s32[5]{0:T(128)}, u32[]{:S(2)}) copy-start(s32[5]{0:T(128)} %bond_ref.1) | copy-start | bytes 64
  4.2 0.7 %copy-start.5 = (f32[5]{0:T(128)S(1)}, f32[5]{0:T(128)}, u32[]{:S(2)}) copy-start(f32[5]{0:T(128)} %strength_ref.1) | copy-start | bytes 64

commit v2 on v1

--- a/solution.py
+++ b/solution.py
@@ -150,13 +150,17 @@
 
 def step_kernel(
     sizes,
+    kind_hbm,
+    bond_hbm,
+    strength_hbm,
+    drive_hbm,
+    amp_ref,
+    coup_ref,
+    out_ref,
     kind_ref,
     bond_ref,
     strength_ref,
     drive_ref,
-    amp_ref,
-    coup_ref,
-    out_ref,
     stage,
     held,
     table,
@@ -185,8 +189,6 @@
         other = lax.rem(me + hop, devices)
         return other, (other // dev_size, lax.rem(other, dev_size))
 
-    load_table = pltpu.make_async_copy(coup_ref, table, local_sem.at[0])
-    load_table.start()
     barrier = pltpu.get_barrier_semaphore()
 
     def greet(hop, carry):
@@ -194,13 +196,28 @@
         return carry
 
     lax.fori_loop(1, devices, greet, 0)
-    stage[0] = amp_ref[0]
-    stage[1] = amp_ref[1]
+    loads = [
+        pltpu.make_async_copy(source, target, local_sem.at[3 + index])
+        for index, (source, target) in enumerate(
+            (
+                (kind_hbm, kind_ref),
+                (amp_ref, stage.at[pl.ds(0, 2)]),
+                (coup_ref, table),
+                (bond_hbm, bond_ref),
+                (strength_hbm, strength_ref),
+                (drive_hbm, drive_ref),
+            )
+        )
+    ]
+    for load in loads:
+        load.start()
+    loads[0].wait()
     for block in range(row_count // block_rows):
         kind = kind_ref[block].astype(jnp.float32)
         stage[2, block * block_rows : (block + 1) * block_rows] = jnp.full(
             (block_rows, col_count), kind, jnp.float32
         )
+    loads[1].wait()
     pl.semaphore_wait(barrier, devices - 1)
 
     mine = pl.ds(me * share, share)
@@ -220,7 +237,7 @@
 
         lax.fori_loop(1, devices, send, 0)
         own = pltpu.make_async_copy(
-            source.at[:, mine], target.at[:, mine], local_sem.at[1 + phase]
+            source.at[:, mine], target.at[:, mine], local_sem.at[phase]
         )
         own.start()
         return own
@@ -233,7 +250,8 @@
         pltpu.make_async_copy(came, came, recv_sem.at[phase]).wait()
 
     own = exchange(stage, held, 0)
-    load_table.wait()
+    for load in loads[2:]:
+        load.wait()
 
     def split(kind, carry):
         real = table[0, kind]
@@ -329,15 +347,17 @@
     kinds = couplings.shape[1]
     block_rows = row_count // block_index.shape[0]
     half = (parts, row_count, col_count)
-    smem = pl.BlockSpec(memory_space=pltpu.SMEM)
-    vmem = pl.BlockSpec(memory_space=pltpu.VMEM)
     weight = pltpu.VMEM((kinds * 2 * col_count, 2 * col_count), jnp.bfloat16)
     return pl.pallas_call(
         functools.partial(step_kernel, (*sizes, block_rows)),
         out_shape=jax.ShapeDtypeStruct(half, jnp.float32),
-        in_specs=[smem, smem, smem, smem, vmem, pl.BlockSpec(memory_space=pl.ANY)],
-        out_specs=vmem,
+        in_specs=[pl.BlockSpec(memory_space=pl.ANY)] * 6,
+        out_specs=pl.BlockSpec(memory_space=pltpu.VMEM),
         scratch_shapes=[
+            pltpu.SMEM(block_index.shape, jnp.int32),
+            pltpu.SMEM(bond_map.shape, jnp.int32),
+            pltpu.SMEM(bond_strength.shape, jnp.float32),
+            pltpu.SMEM(drive_amplitude.shape, jnp.float32),
             pltpu.VMEM((parts + 1, row_count, col_count), jnp.float32),
             pltpu.VMEM((parts + 1, row_count, col_count), jnp.float32),
             pltpu.VMEM(couplings.shape, jnp.float32),
@@ -348,13 +368,11 @@
             pltpu.VMEM(half, jnp.float32),
             pltpu.VMEM(half, jnp.float32),
             pltpu.VMEM(half, jnp.float32),
-            pltpu.SemaphoreType.DMA((3,)),
+            pltpu.SemaphoreType.DMA((9,)),
             pltpu.SemaphoreType.DMA((2,)),
             pltpu.SemaphoreType.DMA((2,)),
         ],
-        compiler_params=pltpu.CompilerParams(
-            collective_id=0, has_side_effects=True, vmem_limit_bytes=32 * 2**20
-        ),
+        compiler_params=pltpu.CompilerParams(collective_id=0, has_side_effects=True),
     )(block_index, bond_map, bond_strength, drive_amplitude, amplitudes, couplings)
 
 

time: 26.1 us -> 21.7 us (0.83)
  local copies, waits for them, and re-layouts: 5.52 us -> 1.47 us
    unnamed x13 -> x1, local copies, waits for them, and re-layouts: 5.52 us -> 1.47 us
where the time goes in v2:
time: 21.7 us; the launch traced here: 21.6 us
  Pallas kernels  20.1 us (93%)
  local copies, waits for them, and re-layouts  1.47 us (7%)
    pallas_call x1, Pallas kernels, body_by_rows(): pl.pallas_call(functools.partial(step_kernel, (*sizes, block_rows)), out_...  20.1 us
    unnamed x1, local copies, waits for them, and re-layouts  1.47 us

profile of v2, /device:TPU:0, one launch (start us, length us, event | category | flops | bytes accessed | tf_op | source)
XLA Modules:
  0.0 21.6 jit_solution(9472758696921342818)
XLA Ops:
  0.0 20.1 %shard_map.64 = f32[2,64,128]{2,1,0:T(8,128)} custom-call(s32[4]{0:T(128)} %kind_hbm.1, s32[5]{0:T(128)} %bond_hbm.1, f32[5]{0:T(128)} %strength_hbm.1, f32[4,5]{1,0:T(4,128)} %drive_hbm.1, f32[2,64,128]{2,1,0:T(8,128)} %amp_ref.1, f32[2,12,128,128]{3,2,1,0:T(8,128)} %coup_ref.1), custom_call_target="tpu_custom_call" | custom-call | tf_op jit(solution)/shard_map/pallas_call | solution.py:351
  20.1 1.5 %copy.8 = f32[2,64,128]{2,1,0:T(8,128)} copy(f32[2,64,128]{2,1,0:T(8,128)} %shard_map.64) | data formatting | bytes 131072

commit v3 on v2

--- a/solution.py
+++ b/solution.py
@@ -131,6 +131,7 @@
 
 
 SUBLANES = 8
+VMEM_GRANT = 64 * 2**20 - 2**18
 MESH = pl.DeviceIdType.MESH
 
 
@@ -191,11 +192,8 @@
 
     barrier = pltpu.get_barrier_semaphore()
 
-    def greet(hop, carry):
+    for hop in range(1, devices):
         pl.semaphore_signal(barrier, inc=1, device_id=place(hop)[1], device_id_type=MESH)
-        return carry
-
-    lax.fori_loop(1, devices, greet, 0)
     loads = [
         pltpu.make_async_copy(source, target, local_sem.at[3 + index])
         for index, (source, target) in enumerate(
@@ -223,7 +221,7 @@
     mine = pl.ds(me * share, share)
 
     def exchange(source, target, phase):
-        def send(hop, carry):
+        for hop in range(1, devices):
             other, where = place(hop)
             pltpu.make_async_remote_copy(
                 src_ref=source.at[:, pl.ds(other * share, share)],
@@ -233,9 +231,6 @@
                 device_id=where,
                 device_id_type=MESH,
             ).start()
-            return carry
-
-        lax.fori_loop(1, devices, send, 0)
         own = pltpu.make_async_copy(
             source.at[:, mine], target.at[:, mine], local_sem.at[phase]
         )
@@ -254,22 +249,13 @@
         load.wait()
 
     def split(kind, carry):
-        real = table[0, kind]
-        imag = table[1, kind]
-        real_high = real.astype(jnp.bfloat16)
-        imag_high = imag.astype(jnp.bfloat16)
-        real_low = (real - real_high.astype(jnp.float32)).astype(jnp.bfloat16)
-        imag_low = (imag - imag_high.astype(jnp.float32)).astype(jnp.bfloat16)
-        first = pl.ds(pl.multiple_of(kind * 2 * col_count, 2 * col_count), col_count)
-        second = pl.ds(pl.multiple_of(kind * 2 * col_count, col_count) + col_count, col_count)
-        for weight, real_now, imag_now in (
-            (weight_high, real_high, imag_high),
-            (weight_low, real_low, imag_low),
-        ):
-            weight[first, :col_count] = -imag_now
-            weight[first, col_count:] = -real_now
-            weight[second, :col_count] = real_now
-            weight[second, col_count:] = -imag_now
+        rows = pl.ds(pl.multiple_of(kind * col_count, col_count), col_count)
+        for part in range(2):
+            columns = slice(part * col_count, (part + 1) * col_count)
+            full = table[part, kind]
+            high = full.astype(jnp.bfloat16)
+            weight_high[rows, columns] = high
+            weight_low[rows, columns] = (full - high.astype(jnp.float32)).astype(jnp.bfloat16)
         return carry
 
     lax.fori_loop(0, kinds, split, 0)
@@ -296,13 +282,13 @@
     total[...] = jnp.zeros_like(total)
 
     def section(now, carry):
-        both = jnp.concatenate([field[0], field[1]], 1)
+        both = jnp.concatenate([field[0], field[1]], 0)
         high = both.astype(jnp.bfloat16)
         low = (both - high.astype(jnp.float32)).astype(jnp.bfloat16)
         high_parts = []
         low_parts = []
         for kind in range(kinds):
-            mask = jnp.concatenate([masks[kind], masks[kind]], 1)
+            mask = jnp.concatenate([masks[kind], masks[kind]], 0)
             high_parts.append(high * mask)
             low_parts.append(low * mask)
         high_all = jnp.concatenate(high_parts, 1)
@@ -313,7 +299,10 @@
             preferred_element_type=jnp.float32,
         )
         rest = jnp.dot(high_all, weight_low[...], preferred_element_type=jnp.float32)
-        product = main[:row_count] + (main[row_count:] + rest)
+        product = main[: 2 * row_count] + (main[2 * row_count :] + rest)
+        from_real, from_imag = product[:row_count], product[row_count:]
+        column_real = from_imag[:, :col_count] - from_real[:, col_count:]
+        column_imag = -from_real[:, :col_count] - from_imag[:, col_count:]
         leads = []
         for part in range(2):
             here = field[part]
@@ -325,7 +314,7 @@
                 )
                 other = other + strength_ref[spin] * moved + drive_ref[now, spin] * there
             leads.append(other)
-        slope = (product[:, :col_count] + leads[1], product[:, col_count:] - leads[0])
+        slope = (column_real + leads[1], column_imag - leads[0])
         edge = (now == 0) | (now == sections - 1)
         weight = jnp.where(edge, 1.0, 2.0)
         step = jnp.where(now == sections - 2, STEP_SIZE, 0.5 * STEP_SIZE)
@@ -347,11 +336,11 @@
     kinds = couplings.shape[1]
     block_rows = row_count // block_index.shape[0]
     half = (parts, row_count, col_count)
-    weight = pltpu.VMEM((kinds * 2 * col_count, 2 * col_count), jnp.bfloat16)
+    weight = pltpu.VMEM((kinds * col_count, 2 * col_count), jnp.bfloat16)
     return pl.pallas_call(
         functools.partial(step_kernel, (*sizes, block_rows)),
-        out_shape=jax.ShapeDtypeStruct(half, jnp.float32),
-        in_specs=[pl.BlockSpec(memory_space=pl.ANY)] * 6,
+        out_shape=pltpu.VMEM(half, jnp.float32),
+        in_specs=[pl.BlockSpec(memory_space=pltpu.HBM)] * 6,
         out_specs=pl.BlockSpec(memory_space=pltpu.VMEM),
         scratch_shapes=[
             pltpu.SMEM(block_index.shape, jnp.int32),
@@ -372,7 +361,9 @@
             pltpu.SemaphoreType.DMA((2,)),
             pltpu.SemaphoreType.DMA((2,)),
         ],
-        compiler_params=pltpu.CompilerParams(collective_id=0, has_side_effects=True),
+        compiler_params=pltpu.CompilerParams(
+            collective_id=0, has_side_effects=True, vmem_limit_bytes=VMEM_GRANT
+        ),
     )(block_index, bond_map, bond_strength, drive_amplitude, amplitudes, couplings)
 
 

time: 21.7 us -> 19.6 us (0.903)
  Pallas kernels: 20.1 us -> 18.8 us
  local copies, waits for them, and re-layouts: 1.47 us -> 0.63 us
    pallas_call x1, Pallas kernels: 20.1 us -> 18.8 us  [body_by_rows(): pl.pallas_call(functools.partial(step_kernel, (*sizes, block_rows)), out_...]
    unnamed x1, local copies, waits for them, and re-layouts: 1.47 us -> 0.63 us
where the time goes in v3:
time: 19.6 us; the launch traced here: 19.5 us
  Pallas kernels  18.8 us (96%)
  local copies, waits for them, and re-layouts  0.63 us (3%)
    pallas_call x1, Pallas kernels, body_by_rows(): pl.pallas_call(functools.partial(step_kernel, (*sizes, block_rows)), out_...  18.8 us
    unnamed x1, local copies, waits for them, and re-layouts  0.63 us

profile of v3, /device:TPU:0, one launch (start us, length us, event | category | flops | bytes accessed | tf_op | source)
XLA Modules:
  0.0 19.5 jit_solution(8042765107432868328)
XLA Ops:
  0.0 18.8 %shard_map.64 = f32[2,64,128]{2,1,0:T(8,128)S(1)} custom-call(s32[4]{0:T(128)} %kind_hbm.1, s32[5]{0:T(128)} %bond_hbm.1, f32[5]{0:T(128)} %strength_hbm.1, f32[4,5]{1,0:T(4,128)} %drive_hbm.1, f32[2,64,128]{2,1,0:T(8,128)} %amp_ref.1, f32[2,12,128,128]{3,2,1,0:T(8,128)} %coup_ref.1), custom_call_target="tpu_custom_call" | custom-call | tf_op jit(solution)/shard_map/pallas_call | solution.py:340
  18.8 0.6 %copy.8 = f32[2,64,128]{2,1,0:T(8,128)} copy(f32[2,64,128]{2,1,0:T(8,128)S(1)} %shard_map.64) | data formatting | bytes 131072

commit v4 on v3

--- a/solution.py
+++ b/solution.py
@@ -172,6 +172,9 @@
     field,
     total,
     final,
+    psi,
+    back,
+    landed,
     local_sem,
     send_sem,
     recv_sem,
@@ -179,11 +182,11 @@
     grp_size, dev_size, block_rows = sizes
     devices = grp_size * dev_size
     lead = spin_count(devices)
-    row_count, col_count = amp_ref.shape[1:]
+    parts, row_count, col_count = amp_ref.shape
     kinds = coup_ref.shape[1]
     sections = drive_ref.shape[0]
     share = row_count // devices
-    others = (devices - 1) * share
+    planes = parts * share
     me = lax.axis_index("grp") * dev_size + lax.axis_index("dev")
 
     def place(hop):
@@ -199,7 +202,7 @@
         for index, (source, target) in enumerate(
             (
                 (kind_hbm, kind_ref),
-                (amp_ref, stage.at[pl.ds(0, 2)]),
+                (amp_ref, final),
                 (coup_ref, table),
                 (bond_hbm, bond_ref),
                 (strength_hbm, strength_ref),
@@ -210,38 +213,42 @@
     for load in loads:
         load.start()
     loads[0].wait()
+    owner = lax.broadcasted_iota(jnp.int32, (devices, col_count), 0) * share // block_rows
+    kind_rows = jnp.zeros((devices, col_count), jnp.float32)
     for block in range(row_count // block_rows):
-        kind = kind_ref[block].astype(jnp.float32)
-        stage[2, block * block_rows : (block + 1) * block_rows] = jnp.full(
-            (block_rows, col_count), kind, jnp.float32
-        )
+        kind_rows = jnp.where(owner == block, kind_ref[block].astype(jnp.float32), kind_rows)
+    stage[pl.ds(planes, devices, stride=planes + 1), :] = kind_rows
     loads[1].wait()
+    for part in range(parts):
+        for spot in range(share):
+            stage[pl.ds(part * share + spot, devices, stride=planes + 1), :] = final[
+                part, pl.ds(spot, devices, stride=share), :
+            ]
     pl.semaphore_wait(barrier, devices - 1)
 
-    mine = pl.ds(me * share, share)
-
     def exchange(source, target, phase):
+        width = source.shape[0] // devices
+        mine = pl.ds(me * width, width)
         for hop in range(1, devices):
             other, where = place(hop)
             pltpu.make_async_remote_copy(
-                src_ref=source.at[:, pl.ds(other * share, share)],
-                dst_ref=target.at[:, mine],
+                src_ref=source.at[pl.ds(other * width, width)],
+                dst_ref=target.at[mine],
                 send_sem=send_sem.at[phase],
                 recv_sem=recv_sem.at[phase],
                 device_id=where,
                 device_id_type=MESH,
             ).start()
-        own = pltpu.make_async_copy(
-            source.at[:, mine], target.at[:, mine], local_sem.at[phase]
-        )
+        own = pltpu.make_async_copy(source.at[mine], target.at[mine], local_sem.at[phase])
         own.start()
         return own
 
     def finish(source, target, phase, own):
         own.wait()
-        sent = source.at[:, pl.ds(0, others)]
+        others = pl.ds(0, source.shape[0] // devices * (devices - 1))
+        sent = source.at[others]
         pltpu.make_async_copy(sent, sent, send_sem.at[phase]).wait()
-        came = target.at[:, pl.ds(0, others)]
+        came = target.at[others]
         pltpu.make_async_copy(came, came, recv_sem.at[phase]).wait()
 
     own = exchange(stage, held, 0)
@@ -268,17 +275,23 @@
         target = bond_ref[spin]
         shuffles.append(jnp.bitwise_xor(column, jnp.left_shift(jnp.int32(1), target)))
         parity = jnp.bitwise_xor(
-            jnp.right_shift(row // share, spin), jnp.right_shift(column, target)
+            jnp.right_shift(row % devices, spin), jnp.right_shift(column, target)
         )
         sign = (1 - 2 * jnp.bitwise_and(parity, 1)).astype(jnp.float32)
         diag = diag + strength_ref[spin] * sign
     diagonal[...] = diag
 
     finish(stage, held, 0, own)
-    kind_rows = held[2]
+    kind_now = held[pl.ds(planes, devices, stride=planes + 1), :]
+    kind_now = jnp.concatenate([kind_now] * share, 0)
     for kind in range(kinds):
-        masks[kind] = (kind_rows == float(kind)).astype(jnp.float32).astype(jnp.bfloat16)
-    field[...] = held[:2]
+        masks[kind] = (kind_now == float(kind)).astype(jnp.float32).astype(jnp.bfloat16)
+    for part in range(parts):
+        for spot in range(share):
+            came = held[pl.ds(part * share + spot, devices, stride=planes + 1), :]
+            rows = slice(spot * devices, (spot + 1) * devices)
+            psi[part, rows] = came
+            field[part, rows] = came
     total[...] = jnp.zeros_like(total)
 
     def section(now, carry):
@@ -308,7 +321,7 @@
             here = field[part]
             other = diagonal[...] * here
             for spin in range(lead):
-                there = flipped(here, share << spin)
+                there = flipped(here, 1 << spin)
                 moved = jnp.take_along_axis(
                     there, shuffles[spin], axis=1, mode="promise_in_bounds"
                 )
@@ -320,13 +333,23 @@
         step = jnp.where(now == sections - 2, STEP_SIZE, 0.5 * STEP_SIZE)
         for part in range(2):
             total[part] = total[part] + weight * slope[part]
-            field[part] = held[part] + step * slope[part]
+            field[part] = psi[part] + step * slope[part]
         return carry
 
     lax.fori_loop(0, sections, section, 0)
-    final[...] = held[:2] + (STEP_SIZE / 6.0) * total[...]
-    own = exchange(final, out_ref, 1)
-    finish(final, out_ref, 1, own)
+    final[...] = psi[...] + (STEP_SIZE / 6.0) * total[...]
+    for part in range(parts):
+        for spot in range(share):
+            back[pl.ds(part * share + spot, devices, stride=planes), :] = final[
+                part, spot * devices : (spot + 1) * devices
+            ]
+    own = exchange(back, landed, 1)
+    finish(back, landed, 1, own)
+    for part in range(parts):
+        for spot in range(share):
+            out_ref[part, pl.ds(spot, devices, stride=share), :] = landed[
+                pl.ds(part * share + spot, devices, stride=planes), :
+            ]
 
 
 def body_by_rows(
@@ -337,6 +360,8 @@
     block_rows = row_count // block_index.shape[0]
     half = (parts, row_count, col_count)
     weight = pltpu.VMEM((kinds * col_count, 2 * col_count), jnp.bfloat16)
+    homeward = pltpu.VMEM((parts * row_count, col_count), jnp.float32)
+    outward = pltpu.VMEM((parts * row_count + sizes[0] * sizes[1], col_count), jnp.float32)
     return pl.pallas_call(
         functools.partial(step_kernel, (*sizes, block_rows)),
         out_shape=pltpu.VMEM(half, jnp.float32),
@@ -347,8 +372,8 @@
             pltpu.SMEM(bond_map.shape, jnp.int32),
             pltpu.SMEM(bond_strength.shape, jnp.float32),
             pltpu.SMEM(drive_amplitude.shape, jnp.float32),
-            pltpu.VMEM((parts + 1, row_count, col_count), jnp.float32),
-            pltpu.VMEM((parts + 1, row_count, col_count), jnp.float32),
+            outward,
+            outward,
             pltpu.VMEM(couplings.shape, jnp.float32),
             weight,
             weight,
@@ -357,6 +382,9 @@
             pltpu.VMEM(half, jnp.float32),
             pltpu.VMEM(half, jnp.float32),
             pltpu.VMEM(half, jnp.float32),
+            pltpu.VMEM(half, jnp.float32),
+            homeward,
+            homeward,
             pltpu.SemaphoreType.DMA((9,)),
             pltpu.SemaphoreType.DMA((2,)),
             pltpu.SemaphoreType.DMA((2,)),

time: 19.6 us -> 19.4 us (0.990)
  Pallas kernels: 18.8 us -> 18.6 us
    pallas_call x1, Pallas kernels: 18.8 us -> 18.6 us  [body_by_rows(): pl.pallas_call(functools.partial(step_kernel, (*sizes, block_rows)), out_...]
where the time goes in v4:
time: 19.4 us; the launch traced here: 19.2 us
  Pallas kernels  18.6 us (96%)
  local copies, waits for them, and re-layouts  0.63 us (3%)
    pallas_call x1, Pallas kernels, body_by_rows(): pl.pallas_call(functools.partial(step_kernel, (*sizes, block_rows)), out_...  18.6 us
    unnamed x1, local copies, waits for them, and re-layouts  0.63 us

profile of v4, /device:TPU:0, one launch (start us, length us, event | category | flops | bytes accessed | tf_op | source)
XLA Modules:
  0.0 19.2 jit_solution(3260568372560634496)
XLA Ops:
  0.0 18.6 %shard_map.64 = f32[2,64,128]{2,1,0:T(8,128)S(1)} custom-call(s32[4]{0:T(128)} %kind_hbm.1, s32[5]{0:T(128)} %bond_hbm.1, f32[5]{0:T(128)} %strength_hbm.1, f32[4,5]{1,0:T(4,128)} %drive_hbm.1, f32[2,64,128]{2,1,0:T(8,128)} %amp_ref.1, f32[2,12,128,128]{3,2,1,0:T(8,128)} %coup_ref.1), custom_call_target="tpu_custom_call" | custom-call | tf_op jit(solution)/shard_map/pallas_call | solution.py:365
  18.6 0.6 %copy.8 = f32[2,64,128]{2,1,0:T(8,128)} copy(f32[2,64,128]{2,1,0:T(8,128)S(1)} %shard_map.64) | data formatting | bytes 131072

commit v5 on v4

--- a/solution.py
+++ b/solution.py
@@ -189,14 +189,14 @@
     planes = parts * share
     me = lax.axis_index("grp") * dev_size + lax.axis_index("dev")
 
+    hops = sorted(
+        range(1, devices), key=lambda hop: -min(hop % dev_size, dev_size - hop % dev_size)
+    )
+
     def place(hop):
         other = lax.rem(me + hop, devices)
         return other, (other // dev_size, lax.rem(other, dev_size))
 
-    barrier = pltpu.get_barrier_semaphore()
-
-    for hop in range(1, devices):
-        pl.semaphore_signal(barrier, inc=1, device_id=place(hop)[1], device_id_type=MESH)
     loads = [
         pltpu.make_async_copy(source, target, local_sem.at[3 + index])
         for index, (source, target) in enumerate(
@@ -212,6 +212,10 @@
     ]
     for load in loads:
         load.start()
+    barrier = pltpu.get_barrier_semaphore()
+
+    for hop in hops:
+        pl.semaphore_signal(barrier, inc=1, device_id=place(hop)[1], device_id_type=MESH)
     loads[0].wait()
     owner = lax.broadcasted_iota(jnp.int32, (devices, col_count), 0) * share // block_rows
     kind_rows = jnp.zeros((devices, col_count), jnp.float32)
@@ -229,7 +233,7 @@
     def exchange(source, target, phase):
         width = source.shape[0] // devices
         mine = pl.ds(me * width, width)
-        for hop in range(1, devices):
+        for hop in hops:
             other, where = place(hop)
             pltpu.make_async_remote_copy(
                 src_ref=source.at[pl.ds(other * width, width)],
@@ -298,21 +302,21 @@
         both = jnp.concatenate([field[0], field[1]], 0)
         high = both.astype(jnp.bfloat16)
         low = (both - high.astype(jnp.float32)).astype(jnp.bfloat16)
-        high_parts = []
-        low_parts = []
-        for kind in range(kinds):
-            mask = jnp.concatenate([masks[kind], masks[kind]], 0)
-            high_parts.append(high * mask)
-            low_parts.append(low * mask)
-        high_all = jnp.concatenate(high_parts, 1)
-        low_all = jnp.concatenate(low_parts, 1)
-        main = jnp.dot(
-            jnp.concatenate([high_all, low_all], 0),
-            weight_high[...],
-            preferred_element_type=jnp.float32,
-        )
-        rest = jnp.dot(high_all, weight_low[...], preferred_element_type=jnp.float32)
-        product = main[: 2 * row_count] + (main[2 * row_count :] + rest)
+        product = jnp.zeros((2 * row_count, 2 * col_count), jnp.float32)
+        for first in range(0, kinds, 2):
+            group = range(first, min(first + 2, kinds))
+            rows = slice(first * col_count, (group[-1] + 1) * col_count)
+            chosen = [jnp.concatenate([masks[kind], masks[kind]], 0) for kind in group]
+            high_now = jnp.concatenate([high * mask for mask in chosen], 1)
+            low_now = jnp.concatenate([low * mask for mask in chosen], 1)
+            for left, right in (
+                (high_now, weight_high),
+                (low_now, weight_high),
+                (high_now, weight_low),
+            ):
+                product = product + jnp.dot(
+                    left, right[rows], preferred_element_type=jnp.float32
+                )
         from_real, from_imag = product[:row_count], product[row_count:]
         column_real = from_imag[:, :col_count] - from_real[:, col_count:]
         column_imag = -from_real[:, :col_count] - from_imag[:, col_count:]

time: 19.4 us -> 20.1 us (1.036)
  Pallas kernels: 18.6 us -> 19.3 us
    pallas_call x1, Pallas kernels: 18.6 us -> 19.3 us  [body_by_rows(): pl.pallas_call(functools.partial(step_kernel, (*sizes, block_rows)), out_...]
where the time goes in v5:
time: 20.1 us; the launch traced here: 19.9 us
  Pallas kernels  19.3 us (96%)
  local copies, waits for them, and re-layouts  0.63 us (3%)
    pallas_call x1, Pallas kernels, body_by_rows(): pl.pallas_call(functools.partial(step_kernel, (*sizes, block_rows)), out_...  19.3 us
    unnamed x1, local copies, waits for them, and re-layouts  0.63 us

profile of v5, /device:TPU:0, one launch (start us, length us, event | category | flops | bytes accessed | tf_op | source)
XLA Modules:
  0.0 19.9 jit_solution(3660790108731231212)
XLA Ops:
  0.0 19.3 %shard_map.64 = f32[2,64,128]{2,1,0:T(8,128)S(1)} custom-call(s32[4]{0:T(128)} %kind_hbm.1, s32[5]{0:T(128)} %bond_hbm.1, f32[5]{0:T(128)} %strength_hbm.1, f32[4,5]{1,0:T(4,128)} %drive_hbm.1, f32[2,64,128]{2,1,0:T(8,128)} %amp_ref.1, f32[2,12,128,128]{3,2,1,0:T(8,128)} %coup_ref.1), custom_call_target="tpu_custom_call" | custom-call | tf_op jit(solution)/shard_map/pallas_call | solution.py:369
  19.3 0.6 %copy.8 = f32[2,64,128]{2,1,0:T(8,128)} copy(f32[2,64,128]{2,1,0:T(8,128)S(1)} %shard_map.64) | data formatting | bytes 131072

commit v6 on v4

--- a/solution.py
+++ b/solution.py
@@ -187,16 +187,17 @@
     sections = drive_ref.shape[0]
     share = row_count // devices
     planes = parts * share
-    me = lax.axis_index("grp") * dev_size + lax.axis_index("dev")
-
-    def place(hop):
-        other = lax.rem(me + hop, devices)
-        return other, (other // dev_size, lax.rem(other, dev_size))
-
-    barrier = pltpu.get_barrier_semaphore()
-
-    for hop in range(1, devices):
-        pl.semaphore_signal(barrier, inc=1, device_id=place(hop)[1], device_id_type=MESH)
+    grp, dev = lax.axis_index("grp"), lax.axis_index("dev")
+    me = grp * dev_size + dev
+    grps = [grp] + [lax.rem(grp + hop, grp_size) for hop in range(1, grp_size)]
+    devs = [dev] + [lax.rem(dev + hop, dev_size) for hop in range(1, dev_size)]
+    hops = sorted(range(dev_size), key=lambda hop: -min(hop, dev_size - hop))
+    others = [
+        (grps[grp_hop] * dev_size + devs[dev_hop], (grps[grp_hop], devs[dev_hop]))
+        for dev_hop in hops
+        for grp_hop in reversed(range(grp_size))
+        if grp_hop + dev_hop > 0
+    ]
     loads = [
         pltpu.make_async_copy(source, target, local_sem.at[3 + index])
         for index, (source, target) in enumerate(
@@ -210,7 +211,13 @@
             )
         )
     ]
-    for load in loads:
+    for load in loads[:2]:
+        load.start()
+    barrier = pltpu.get_barrier_semaphore()
+
+    for _, where in others:
+        pl.semaphore_signal(barrier, inc=1, device_id=where, device_id_type=MESH)
+    for load in loads[2:]:
         load.start()
     loads[0].wait()
     owner = lax.broadcasted_iota(jnp.int32, (devices, col_count), 0) * share // block_rows
@@ -229,8 +236,7 @@
     def exchange(source, target, phase):
         width = source.shape[0] // devices
         mine = pl.ds(me * width, width)
-        for hop in range(1, devices):
-            other, where = place(hop)
+        for other, where in others:
             pltpu.make_async_remote_copy(
                 src_ref=source.at[pl.ds(other * width, width)],
                 dst_ref=target.at[mine],
@@ -245,10 +251,10 @@
 
     def finish(source, target, phase, own):
         own.wait()
-        others = pl.ds(0, source.shape[0] // devices * (devices - 1))
-        sent = source.at[others]
+        foreign = pl.ds(0, source.shape[0] // devices * (devices - 1))
+        sent = source.at[foreign]
         pltpu.make_async_copy(sent, sent, send_sem.at[phase]).wait()
-        came = target.at[others]
+        came = target.at[foreign]
         pltpu.make_async_copy(came, came, recv_sem.at[phase]).wait()
 
     own = exchange(stage, held, 0)

time: 19.4 us -> 19.8 us (1.021)
  Pallas kernels: 18.6 us -> 19 us
    pallas_call x1, Pallas kernels: 18.6 us -> 19 us  [body_by_rows(): pl.pallas_call(functools.partial(step_kernel, (*sizes, block_rows)), out_...]
where the time goes in v6:
time: 19.8 us; the launch traced here: 19.7 us
  Pallas kernels  19 us (96%)
  local copies, waits for them, and re-layouts  0.63 us (3%)
    pallas_call x1, Pallas kernels, body_by_rows(): pl.pallas_call(functools.partial(step_kernel, (*sizes, block_rows)), out_...  19 us
    unnamed x1, local copies, waits for them, and re-layouts  0.63 us

profile of v6, /device:TPU:0, one launch (start us, length us, event | category | flops | bytes accessed | tf_op | source)
XLA Modules:
  0.0 19.7 jit_solution(7480107256464549228)
XLA Ops:
  0.0 19.0 %shard_map.64 = f32[2,64,128]{2,1,0:T(8,128)S(1)} custom-call(s32[4]{0:T(128)} %kind_hbm.1, s32[5]{0:T(128)} %bond_hbm.1, f32[5]{0:T(128)} %strength_hbm.1, f32[4,5]{1,0:T(4,128)} %drive_hbm.1, f32[2,64,128]{2,1,0:T(8,128)} %amp_ref.1, f32[2,12,128,128]{3,2,1,0:T(8,128)} %coup_ref.1), custom_call_target="tpu_custom_call" | custom-call | tf_op jit(solution)/shard_map/pallas_call | solution.py:371
  19.0 0.6 %copy.8 = f32[2,64,128]{2,1,0:T(8,128)} copy(f32[2,64,128]{2,1,0:T(8,128)S(1)} %shard_map.64) | data formatting | bytes 131072

commit v7 on v6

--- a/solution.py
+++ b/solution.py
@@ -147,6 +147,13 @@
         up = pltpu.roll(tiles, SUBLANES - stride, 1)
         down = jnp.where(row // stride % 2 == 1, down, up)
     return down.reshape(row_count, col_count)
+
+
+def mixed_order(count):
+    order = [0]
+    while len(order) < count:
+        order = [2 * place for place in order] + [2 * place + 1 for place in order]
+    return order
 
 
 def step_kernel(
@@ -191,11 +198,11 @@
     me = grp * dev_size + dev
     grps = [grp] + [lax.rem(grp + hop, grp_size) for hop in range(1, grp_size)]
     devs = [dev] + [lax.rem(dev + hop, dev_size) for hop in range(1, dev_size)]
-    hops = sorted(range(dev_size), key=lambda hop: -min(hop, dev_size - hop))
+    hops = mixed_order(dev_size)
     others = [
         (grps[grp_hop] * dev_size + devs[dev_hop], (grps[grp_hop], devs[dev_hop]))
+        for grp_hop in reversed(range(grp_size))
         for dev_hop in hops
-        for grp_hop in reversed(range(grp_size))
         if grp_hop + dev_hop > 0
     ]
     loads = [

time: 19.8 us -> 19.2 us (0.970)
  Pallas kernels: 19 us -> 18.4 us
    pallas_call x1, Pallas kernels: 19 us -> 18.4 us  [body_by_rows(): pl.pallas_call(functools.partial(step_kernel, (*sizes, block_rows)), out_...]
where the time goes in v7:
time: 19.2 us; the launch traced here: 19 us
  Pallas kernels  18.4 us (96%)
  local copies, waits for them, and re-layouts  0.63 us (3%)
    pallas_call x1, Pallas kernels, body_by_rows(): pl.pallas_call(functools.partial(step_kernel, (*sizes, block_rows)), out_...  18.4 us
    unnamed x1, local copies, waits for them, and re-layouts  0.63 us

profile of v7, /device:TPU:0, one launch (start us, length us, event | category | flops | bytes accessed | tf_op | source)
XLA Modules:
  0.0 19.0 jit_solution(16434338958085809850)
XLA Ops:
  0.0 18.4 %shard_map.64 = f32[2,64,128]{2,1,0:T(8,128)S(1)} custom-call(s32[4]{0:T(128)} %kind_hbm.1, s32[5]{0:T(128)} %bond_hbm.1, f32[5]{0:T(128)} %strength_hbm.1, f32[4,5]{1,0:T(4,128)} %drive_hbm.1, f32[2,64,128]{2,1,0:T(8,128)} %amp_ref.1, f32[2,12,128,128]{3,2,1,0:T(8,128)} %coup_ref.1), custom_call_target="tpu_custom_call" | custom-call | tf_op jit(solution)/shard_map/pallas_call | solution.py:378
  18.4 0.6 %copy.8 = f32[2,64,128]{2,1,0:T(8,128)} copy(f32[2,64,128]{2,1,0:T(8,128)S(1)} %shard_map.64) | data formatting | bytes 131072

commit v8 on v6

--- a/solution.py
+++ b/solution.py
@@ -189,15 +189,16 @@
     planes = parts * share
     grp, dev = lax.axis_index("grp"), lax.axis_index("dev")
     me = grp * dev_size + dev
-    grps = [grp] + [lax.rem(grp + hop, grp_size) for hop in range(1, grp_size)]
-    devs = [dev] + [lax.rem(dev + hop, dev_size) for hop in range(1, dev_size)]
-    hops = sorted(range(dev_size), key=lambda hop: -min(hop, dev_size - hop))
-    others = [
-        (grps[grp_hop] * dev_size + devs[dev_hop], (grps[grp_hop], devs[dev_hop]))
-        for dev_hop in hops
-        for grp_hop in reversed(range(grp_size))
-        if grp_hop + dev_hop > 0
-    ]
+
+    def for_others(action):
+        def visit(hop, carry):
+            there = lax.rem(grp + lax.div(hop, dev_size), grp_size)
+            spot = lax.rem(dev + lax.rem(hop, dev_size), dev_size)
+            action(there * dev_size + spot, (there, spot))
+            return carry
+
+        lax.fori_loop(1, devices, visit, 0)
+
     loads = [
         pltpu.make_async_copy(source, target, local_sem.at[3 + index])
         for index, (source, target) in enumerate(
@@ -215,8 +216,11 @@
         load.start()
     barrier = pltpu.get_barrier_semaphore()
 
-    for _, where in others:
-        pl.semaphore_signal(barrier, inc=1, device_id=where, device_id_type=MESH)
+    for_others(
+        lambda _, where: pl.semaphore_signal(
+            barrier, inc=1, device_id=where, device_id_type=MESH
+        )
+    )
     for load in loads[2:]:
         load.start()
     loads[0].wait()
@@ -236,7 +240,8 @@
     def exchange(source, target, phase):
         width = source.shape[0] // devices
         mine = pl.ds(me * width, width)
-        for other, where in others:
+
+        def send(other, where):
             pltpu.make_async_remote_copy(
                 src_ref=source.at[pl.ds(other * width, width)],
                 dst_ref=target.at[mine],
@@ -245,6 +250,8 @@
                 device_id=where,
                 device_id_type=MESH,
             ).start()
+
+        for_others(send)
         own = pltpu.make_async_copy(source.at[mine], target.at[mine], local_sem.at[phase])
         own.start()
         return own

time: 19.8 us -> 19.7 us (level)
  no operation moved by 1% of the time
where the time goes in v8:
time: 19.7 us; the launch traced here: 19.6 us
  Pallas kernels  18.9 us (96%)
  local copies, waits for them, and re-layouts  0.63 us (3%)
    pallas_call x1, Pallas kernels, body_by_rows(): pl.pallas_call(functools.partial(step_kernel, (*sizes, block_rows)), out_...  18.9 us
    unnamed x1, local copies, waits for them, and re-layouts  0.63 us

profile of v8, /device:TPU:0, one launch (start us, length us, event | category | flops | bytes accessed | tf_op | source)
XLA Modules:
  0.0 19.6 jit_solution(15205838777556812670)
XLA Ops:
  0.0 18.9 %shard_map.64 = f32[2,64,128]{2,1,0:T(8,128)S(1)} custom-call(s32[4]{0:T(128)} %kind_hbm.1, s32[5]{0:T(128)} %bond_hbm.1, f32[5]{0:T(128)} %strength_hbm.1, f32[4,5]{1,0:T(4,128)} %drive_hbm.1, f32[2,64,128]{2,1,0:T(8,128)} %amp_ref.1, f32[2,12,128,128]{3,2,1,0:T(8,128)} %coup_ref.1), custom_call_target="tpu_custom_call" | custom-call | tf_op jit(solution)/shard_map/pallas_call | solution.py:378
  18.9 0.6 %copy.8 = f32[2,64,128]{2,1,0:T(8,128)} copy(f32[2,64,128]{2,1,0:T(8,128)S(1)} %shard_map.64) | data formatting | bytes 131072

commit v9 on v7

--- a/solution.py
+++ b/solution.py
@@ -198,13 +198,25 @@
     me = grp * dev_size + dev
     grps = [grp] + [lax.rem(grp + hop, grp_size) for hop in range(1, grp_size)]
     devs = [dev] + [lax.rem(dev + hop, dev_size) for hop in range(1, dev_size)]
-    hops = mixed_order(dev_size)
-    others = [
-        (grps[grp_hop] * dev_size + devs[dev_hop], (grps[grp_hop], devs[dev_hop]))
-        for grp_hop in reversed(range(grp_size))
-        for dev_hop in hops
-        if grp_hop + dev_hop > 0
-    ]
+    shift = lax.rem(grp, 2) * (dev_size // 4)
+    turned = [lax.rem(dev + hop + shift, dev_size) for hop in range(dev_size)]
+    others = []
+    for grp_hop in reversed(range(grp_size)):
+        row_of = turned if grp_hop else devs
+        for dev_hop in mixed_order(dev_size):
+            if grp_hop + dev_hop > 0:
+                where = (grps[grp_hop], row_of[dev_hop])
+                others.append((where[0] * dev_size + where[1], where))
+    barrier = pltpu.get_barrier_semaphore()
+    for dev_hop in sorted(range(dev_size), key=lambda hop: -min(hop, dev_size - hop)):
+        for grp_hop in reversed(range(grp_size)):
+            if grp_hop + dev_hop > 0:
+                pl.semaphore_signal(
+                    barrier,
+                    inc=1,
+                    device_id=(grps[grp_hop], devs[dev_hop]),
+                    device_id_type=MESH,
+                )
     loads = [
         pltpu.make_async_copy(source, target, local_sem.at[3 + index])
         for index, (source, target) in enumerate(
@@ -218,13 +230,7 @@
             )
         )
     ]
-    for load in loads[:2]:
-        load.start()
-    barrier = pltpu.get_barrier_semaphore()
-
-    for _, where in others:
-        pl.semaphore_signal(barrier, inc=1, device_id=where, device_id_type=MESH)
-    for load in loads[2:]:
+    for load in loads:
         load.start()
     loads[0].wait()
     owner = lax.broadcasted_iota(jnp.int32, (devices, col_count), 0) * share // block_rows

time: 19.2 us -> 19.2 us (level)
  no operation moved by 1% of the time
where the time goes in v9:
time: 19.2 us; the launch traced here: 19.1 us
  Pallas kernels  18.5 us (96%)
  local copies, waits for them, and re-layouts  0.63 us (3%)
    pallas_call x1, Pallas kernels, body_by_rows(): pl.pallas_call(functools.partial(step_kernel, (*sizes, block_rows)), out_...  18.5 us
    unnamed x1, local copies, waits for them, and re-layouts  0.63 us

profile of v9, /device:TPU:0, one launch (start us, length us, event | category | flops | bytes accessed | tf_op | source)
XLA Modules:
  0.0 19.1 jit_solution(13810307040018378760)
XLA Ops:
  0.0 18.5 %shard_map.64 = f32[2,64,128]{2,1,0:T(8,128)S(1)} custom-call(s32[4]{0:T(128)} %kind_hbm.1, s32[5]{0:T(128)} %bond_hbm.1, f32[5]{0:T(128)} %strength_hbm.1, f32[4,5]{1,0:T(4,128)} %drive_hbm.1, f32[2,64,128]{2,1,0:T(8,128)} %amp_ref.1, f32[2,12,128,128]{3,2,1,0:T(8,128)} %coup_ref.1), custom_call_target="tpu_custom_call" | custom-call | tf_op jit(solution)/shard_map/pallas_call | solution.py:384
  18.5 0.6 %copy.8 = f32[2,64,128]{2,1,0:T(8,128)} copy(f32[2,64,128]{2,1,0:T(8,128)S(1)} %shard_map.64) | data formatting | bytes 131072

commit v10 on v9

--- a/solution.py
+++ b/solution.py
@@ -289,10 +289,14 @@
     row = lax.broadcasted_iota(jnp.int32, (row_count, col_count), 0)
     column = lax.broadcasted_iota(jnp.int32, (row_count, col_count), 1)
     diag = jnp.zeros((row_count, col_count), jnp.float32)
-    shuffles = []
+    entry = lax.broadcasted_iota(jnp.int32, (col_count, col_count), 0)
+    exit_column = lax.broadcasted_iota(jnp.int32, (col_count, col_count), 1)
     for spin in range(lead):
         target = bond_ref[spin]
-        shuffles.append(jnp.bitwise_xor(column, jnp.left_shift(jnp.int32(1), target)))
+        shuffle = entry == jnp.bitwise_xor(exit_column, jnp.left_shift(jnp.int32(1), target))
+        rows = slice((kinds + spin) * col_count, (kinds + spin + 1) * col_count)
+        weight_high[rows, :col_count] = shuffle.astype(jnp.float32).astype(jnp.bfloat16)
+        weight_high[rows, col_count:] = jnp.zeros((col_count, col_count), jnp.bfloat16)
         parity = jnp.bitwise_xor(
             jnp.right_shift(row % devices, spin), jnp.right_shift(column, target)
         )
@@ -323,10 +327,27 @@
             mask = jnp.concatenate([masks[kind], masks[kind]], 0)
             high_parts.append(high * mask)
             low_parts.append(low * mask)
+        others_high = []
+        others_low = []
+        leads = [diagonal[...] * field[part] for part in range(parts)]
+        for spin in range(lead):
+            there = [flipped(field[part], 1 << spin) for part in range(parts)]
+            for part in range(parts):
+                leads[part] = leads[part] + drive_ref[now, spin] * there[part]
+            scaled = strength_ref[spin] * jnp.concatenate(there, 0)
+            scaled_high = scaled.astype(jnp.bfloat16)
+            others_high.append(scaled_high)
+            others_low.append((scaled - scaled_high.astype(jnp.float32)).astype(jnp.bfloat16))
         high_all = jnp.concatenate(high_parts, 1)
-        low_all = jnp.concatenate(low_parts, 1)
+        main_left = jnp.concatenate(
+            [
+                jnp.concatenate(high_parts + others_high, 1),
+                jnp.concatenate(low_parts + others_low, 1),
+            ],
+            0,
+        )
         main = jnp.dot(
-            jnp.concatenate([high_all, low_all], 0),
+            main_left,
             weight_high[...],
             preferred_element_type=jnp.float32,
         )
@@ -335,17 +356,6 @@
         from_real, from_imag = product[:row_count], product[row_count:]
         column_real = from_imag[:, :col_count] - from_real[:, col_count:]
         column_imag = -from_real[:, :col_count] - from_imag[:, col_count:]
-        leads = []
-        for part in range(2):
-            here = field[part]
-            other = diagonal[...] * here
-            for spin in range(lead):
-                there = flipped(here, 1 << spin)
-                moved = jnp.take_along_axis(
-                    there, shuffles[spin], axis=1, mode="promise_in_bounds"
-                )
-                other = other + strength_ref[spin] * moved + drive_ref[now, spin] * there
-            leads.append(other)
         slope = (column_real + leads[1], column_imag - leads[0])
         edge = (now == 0) | (now == sections - 1)
         weight = jnp.where(edge, 1.0, 2.0)
@@ -378,7 +388,7 @@
     kinds = couplings.shape[1]
     block_rows = row_count // block_index.shape[0]
     half = (parts, row_count, col_count)
-    weight = pltpu.VMEM((kinds * col_count, 2 * col_count), jnp.bfloat16)
+    lead = spin_count(sizes[0] * sizes[1])
     homeward = pltpu.VMEM((parts * row_count, col_count), jnp.float32)
     outward = pltpu.VMEM((parts * row_count + sizes[0] * sizes[1], col_count), jnp.float32)
     return pl.pallas_call(
@@ -394,8 +404,8 @@
             outward,
             outward,
             pltpu.VMEM(couplings.shape, jnp.float32),
-            weight,
-            weight,
+            pltpu.VMEM(((kinds + lead) * col_count, 2 * col_count), jnp.bfloat16),
+            pltpu.VMEM((kinds * col_count, 2 * col_count), jnp.bfloat16),
             pltpu.VMEM((kinds, row_count, col_count), jnp.bfloat16),
             pltpu.VMEM((row_count, col_count), jnp.float32),
             pltpu.VMEM(half, jnp.float32),

time: 19.2 us -> 19.6 us (1.021)
  Pallas kernels: 18.5 us -> 18.8 us
    pallas_call x1, Pallas kernels: 18.5 us -> 18.8 us  [body_by_rows(): pl.pallas_call(functools.partial(step_kernel, (*sizes, block_rows)), out_...]
where the time goes in v10:
time: 19.6 us; the launch traced here: 19.5 us
  Pallas kernels  18.8 us (96%)
  local copies, waits for them, and re-layouts  0.63 us (3%)
    pallas_call x1, Pallas kernels, body_by_rows(): pl.pallas_call(functools.partial(step_kernel, (*sizes, block_rows)), out_...  18.8 us
    unnamed x1, local copies, waits for them, and re-layouts  0.63 us

profile of v10, /device:TPU:0, one launch (start us, length us, event | category | flops | bytes accessed | tf_op | source)
XLA Modules:
  0.0 19.5 jit_solution(15427470617492469416)
XLA Ops:
  0.0 18.8 %shard_map.64 = f32[2,64,128]{2,1,0:T(8,128)S(1)} custom-call(s32[4]{0:T(128)} %kind_hbm.1, s32[5]{0:T(128)} %bond_hbm.1, f32[5]{0:T(128)} %strength_hbm.1, f32[4,5]{1,0:T(4,128)} %drive_hbm.1, f32[2,64,128]{2,1,0:T(8,128)} %amp_ref.1, f32[2,12,128,128]{3,2,1,0:T(8,128)} %coup_ref.1), custom_call_target="tpu_custom_call" | custom-call | tf_op jit(solution)/shard_map/pallas_call | solution.py:394
  18.9 0.6 %copy.8 = f32[2,64,128]{2,1,0:T(8,128)} copy(f32[2,64,128]{2,1,0:T(8,128)S(1)} %shard_map.64) | data formatting | bytes 131072

commit v11 on v7

--- a/solution.py
+++ b/solution.py
@@ -307,7 +307,7 @@
             field[part, rows] = came
     total[...] = jnp.zeros_like(total)
 
-    def section(now, carry):
+    def section(now):
         both = jnp.concatenate([field[0], field[1]], 0)
         high = both.astype(jnp.bfloat16)
         low = (both - high.astype(jnp.float32)).astype(jnp.bfloat16)
@@ -341,15 +341,14 @@
                 other = other + strength_ref[spin] * moved + drive_ref[now, spin] * there
             leads.append(other)
         slope = (column_real + leads[1], column_imag - leads[0])
-        edge = (now == 0) | (now == sections - 1)
-        weight = jnp.where(edge, 1.0, 2.0)
-        step = jnp.where(now == sections - 2, STEP_SIZE, 0.5 * STEP_SIZE)
+        weight = 1.0 if now in (0, sections - 1) else 2.0
+        step = STEP_SIZE if now == sections - 2 else 0.5 * STEP_SIZE
         for part in range(2):
             total[part] = total[part] + weight * slope[part]
             field[part] = psi[part] + step * slope[part]
-        return carry
-
-    lax.fori_loop(0, sections, section, 0)
+
+    for now in range(sections):
+        section(now)
     final[...] = psi[...] + (STEP_SIZE / 6.0) * total[...]
     for part in range(parts):
         for spot in range(share):

time: 19.2 us -> 20.1 us (1.047)
  Pallas kernels: 18.4 us -> 19.3 us
    pallas_call x1, Pallas kernels: 18.4 us -> 19.3 us  [body_by_rows(): pl.pallas_call(functools.partial(step_kernel, (*sizes, block_rows)), out_...]
where the time goes in v11:
time: 20.1 us; the launch traced here: 19.9 us
  Pallas kernels  19.3 us (96%)
  local copies, waits for them, and re-layouts  0.63 us (3%)
    pallas_call x1, Pallas kernels, body_by_rows(): pl.pallas_call(functools.partial(step_kernel, (*sizes, block_rows)), out_...  19.3 us
    unnamed x1, local copies, waits for them, and re-layouts  0.63 us

profile of v11, /device:TPU:0, one launch (start us, length us, event | category | flops | bytes accessed | tf_op | source)
XLA Modules:
  0.0 19.9 jit_solution(2309451734596985512)
XLA Ops:
  0.0 19.3 %shard_map.64 = f32[2,64,128]{2,1,0:T(8,128)S(1)} custom-call(s32[4]{0:T(128)} %kind_hbm.1, s32[5]{0:T(128)} %bond_hbm.1, f32[5]{0:T(128)} %strength_hbm.1, f32[4,5]{1,0:T(4,128)} %drive_hbm.1, f32[2,64,128]{2,1,0:T(8,128)} %amp_ref.1, f32[2,12,128,128]{3,2,1,0:T(8,128)} %coup_ref.1), custom_call_target="tpu_custom_call" | custom-call | tf_op jit(solution)/shard_map/pallas_call | solution.py:377
  19.3 0.6 %copy.8 = f32[2,64,128]{2,1,0:T(8,128)} copy(f32[2,64,128]{2,1,0:T(8,128)S(1)} %shard_map.64) | data formatting | bytes 131072

commit v12 on v8

--- a/solution.py
+++ b/solution.py
@@ -147,6 +147,13 @@
         up = pltpu.roll(tiles, SUBLANES - stride, 1)
         down = jnp.where(row // stride % 2 == 1, down, up)
     return down.reshape(row_count, col_count)
+
+
+def mixed_order(count):
+    order = [0]
+    while len(order) < count:
+        order = [2 * place for place in order] + [2 * place + 1 for place in order]
+    return order
 
 
 def step_kernel(
@@ -189,15 +196,21 @@
     planes = parts * share
     grp, dev = lax.axis_index("grp"), lax.axis_index("dev")
     me = grp * dev_size + dev
+    devs = [dev] + [lax.rem(dev + hop, dev_size) for hop in range(1, dev_size)]
 
     def for_others(action):
-        def visit(hop, carry):
-            there = lax.rem(grp + lax.div(hop, dev_size), grp_size)
-            spot = lax.rem(dev + lax.rem(hop, dev_size), dev_size)
-            action(there * dev_size + spot, (there, spot))
+        def visit(there, skipped):
+            for dev_hop in mixed_order(dev_size):
+                if dev_hop >= skipped:
+                    where = (there, devs[dev_hop])
+                    action(where[0] * dev_size + where[1], where)
+
+        def visit_group(hop, carry):
+            visit(lax.rem(grp + hop, grp_size), 0)
             return carry
 
-        lax.fori_loop(1, devices, visit, 0)
+        lax.fori_loop(1, grp_size, visit_group, 0)
+        visit(grp, 1)
 
     loads = [
         pltpu.make_async_copy(source, target, local_sem.at[3 + index])

time: 19.7 us -> 19.3 us (0.980)
  Pallas kernels: 18.9 us -> 18.5 us
    pallas_call x1, Pallas kernels: 18.9 us -> 18.5 us  [body_by_rows(): pl.pallas_call(functools.partial(step_kernel, (*sizes, block_rows)), out_...]
where the time goes in v12:
time: 19.3 us; the launch traced here: 19.1 us
  Pallas kernels  18.5 us (96%)
  local copies, waits for them, and re-layouts  0.63 us (3%)
    pallas_call x1, Pallas kernels, body_by_rows(): pl.pallas_call(functools.partial(step_kernel, (*sizes, block_rows)), out_...  18.5 us
    unnamed x1, local copies, waits for them, and re-layouts  0.63 us

profile of v12, /device:TPU:0, one launch (start us, length us, event | category | flops | bytes accessed | tf_op | source)
XLA Modules:
  0.0 19.1 jit_solution(16399054108136882411)
XLA Ops:
  0.0 18.5 %shard_map.64 = f32[2,64,128]{2,1,0:T(8,128)S(1)} custom-call(s32[4]{0:T(128)} %kind_hbm.1, s32[5]{0:T(128)} %bond_hbm.1, f32[5]{0:T(128)} %strength_hbm.1, f32[4,5]{1,0:T(4,128)} %drive_hbm.1, f32[2,64,128]{2,1,0:T(8,128)} %amp_ref.1, f32[2,12,128,128]{3,2,1,0:T(8,128)} %coup_ref.1), custom_call_target="tpu_custom_call" | custom-call | tf_op jit(solution)/shard_map/pallas_call | solution.py:391
  18.5 0.6 %copy.8 = f32[2,64,128]{2,1,0:T(8,128)} copy(f32[2,64,128]{2,1,0:T(8,128)S(1)} %shard_map.64) | data formatting | bytes 131072
